TPU v7x, 512 devices: a whole 4x8x8 slice. The times are simulated.
512 devices in a mesh: dir: 16 (over y, x_lo), space: 32 (over z, x_hi, core).
Axes of the slice: x: 4 (x_hi: 2, x_lo: 2; x = x_hi * 2 + x_lo), y: 8, z: 8, core: 2. Of those that a mesh axis runs over, the one named last changes fastest.
Arguments:
- velocity: float32 [16, 3, 256, 16, 512], P('dir', None, 'space'), may hold values from -6 to 6
- precursor: float32 [16, 3, 256, 512], P('dir', None, 'space'), may hold values from -6 to 6
- rot_map: int32 [16, 256, 512], P('dir', 'space'), may hold values from 0 to 131071, as said below
- facade_cell: int32 [16, 8192], P('dir', 'space'), may hold values from 0 to 65535
- facade_owner: int32 [16, 8192, 1], P('dir', 'space'), may hold values from 0 to 31; in each aligned block of 256 rows (0 to 255, 256 to 511, ..., all dimensions but the last counted through in order) at most 24 rows name the same one
- facade_panel: int32 [16, 8192], P('dir', 'space'), may hold values from 0 to 127
- facade_area: float32 [16, 8192], P('dir', 'space'), may hold values from 0.2 to 2
Outputs:
- velocity_new: float32 [16, 3, 256, 16, 512], P('dir', None, 'space')
- potential: float32 [16, 256, 16, 512], P('dir', 'space')
- panel_force: float32 [16, 4096], P('dir', 'space')
Inputs may be any that keep to these rules, and one draw needn't show every extreme that they name: rot_map[d, y, z] = q_d(y) * 512 + z, where q_d is a permutation of the 256 spanwise rows, drawn for each direction. `facade_owner`: among the 256 facade cells of one device at most 24 have the same owner.
All inputs are finite; a program needn't handle non-finite values.
Results may differ from a plain program's by a relative error of at most 0.00002.
Values sent between devices are 32-bit elements; how exact they have to be, the bound alone decides.
A program may use at most 192 MiB of HBM per device.

v0:
```python
import jax
import jax.numpy as jnp
from jax import lax
from jax.sharding import PartitionSpec as P

ITERS = 20
PAN_DEV = 128


time_step = 0.12
viscosity = 0.2


def extended_2(cells, sides, width):
    for axis, dim in sides:
        count = lax.axis_size(axis)
        ends = count - 1
        head = lax.slice_in_dim(cells, 0, width, axis=dim)
        tail = lax.slice_in_dim(cells, cells.shape[dim] - width, cells.shape[dim], axis=dim)
        cells = jnp.concatenate(
            [
                lax.ppermute(tail, axis, [(i, (i + 1) % count) for i in range(ends)]),
                cells,
                lax.ppermute(head, axis, [((i + 1) % count, i) for i in range(ends)]),
            ],
            axis=dim,
        )
    return cells


def spread(block, axis, holder):
    block = jnp.where(lax.axis_index(axis) == holder, block, jnp.zeros_like(block))
    return lax.psum(block, axis)


def pad_edges(field):
    lead = field.ndim - 3
    widths = [(0, 0)] * lead
    padded = jnp.pad(field, widths + [(0, 0), (0, 0), (1, 1)])
    return jnp.pad(padded, widths + [(0, 0), (1, 1), (0, 0)], mode="edge")


def tentative(extended):
    q = pad_edges(extended)
    centre = q[:, 1:-1, 1:-1, 1:-1]
    xplus = q[:, 1:-1, 2:, 1:-1]
    xminus = q[:, 1:-1, :-2, 1:-1]
    zplus = q[:, 1:-1, 1:-1, 2:]
    zminus = q[:, 1:-1, 1:-1, :-2]
    yplus = q[:, 2:, 1:-1, 1:-1]
    yminus = q[:, :-2, 1:-1, 1:-1]
    lap = xplus + xminus + zplus + zminus + 16.0 * (yplus + yminus) - 36.0 * centre
    advect = (
        centre[0] * (xplus - xminus) * 0.5
        + centre[1] * (yplus - yminus) * 2.0
        + centre[2] * (zplus - zminus) * 0.5
    )
    return centre + time_step * (viscosity * lap - advect)


def divergence(extended):
    q = pad_edges(extended)
    along_x = (q[0, 1:-1, 2:, 1:-1] - q[0, 1:-1, :-2, 1:-1]) * 0.5
    along_y = (q[1, 2:, 1:-1, 1:-1] - q[1, :-2, 1:-1, 1:-1]) * 2.0
    along_z = (q[2, 1:-1, 1:-1, 2:] - q[2, 1:-1, 1:-1, :-2]) * 0.5
    return along_x + along_y + along_z


def relax_sweep(extended, source):
    q = jnp.pad(extended, ((0, 0), (1, 1), (1, 1)))
    total = q[1:-1, 2:, 1:-1] + q[1:-1, :-2, 1:-1] + q[1:-1, 1:-1, 2:] + q[1:-1, 1:-1, :-2]
    total = total + 16.0 * (q[2:, 1:-1, 1:-1] + q[:-2, 1:-1, 1:-1])
    return (total - source) / 36.0


def gradient(extended):
    q = jnp.pad(extended, ((0, 0), (1, 1), (1, 1)))
    grad_x = (q[1:-1, 2:, 1:-1] - q[1:-1, :-2, 1:-1]) * 0.5
    grad_y = (q[2:, 1:-1, 1:-1] - q[:-2, 1:-1, 1:-1]) * 2.0
    grad_z = (q[1:-1, 1:-1, 2:] - q[1:-1, 1:-1, :-2]) * 0.5
    return jnp.stack([grad_x, grad_y, grad_z])


def extend(field, width):
    return extended_2(field, (("space", 0),), width)


def inside_rows(first, count, span):
    global_rows = first + jnp.arange(count, dtype=jnp.int32)
    return (global_rows >= 0) & (global_rows < span)


def body(velocity, precursor, rot_map, facade_cell, facade_owner, facade_panel, facade_area):
    groups = lax.axis_size("space")
    rows = velocity.shape[2]
    stream = velocity.shape[3]
    height = velocity.shape[4]
    span = rows * groups
    start = lax.axis_index("space") * rows
    plane_piece = spread(precursor, "dir", 0)
    plane = lax.all_gather(plane_piece[0], "space", axis=1, tiled=True)
    flat_plane = plane.reshape(3, span * height)
    inflow = jnp.take(flat_plane, rot_map[0].reshape(-1), axis=1).reshape(3, rows, height)
    field = velocity[0].at[:, :, 0, :].set(inflow)
    sweeps_each = 1
    widened = extended_2(field, (("space", 1),), sweeps_each + 1)
    ustar_wide = tentative(widened)
    keep = inside_rows(start - sweeps_each, rows + 2 * sweeps_each, span)
    ustar_wide = jnp.where(keep[None, :, None, None], ustar_wide, 0.0)
    ustar = ustar_wide[:, sweeps_each : sweeps_each + rows]
    source_wide = divergence(ustar_wide)
    empty = jnp.zeros((rows, stream, height), jnp.float32)

    def one_round(step, phi):
        current = extend(phi, sweeps_each)
        current = relax_sweep(current, source_wide)
        return current

    phi = lax.fori_loop(0, ITERS // sweeps_each, one_round, empty)
    moved = ustar - gradient(extend(phi, 1))
    values = facade_area[0] * phi.reshape(-1)[facade_cell[0]]
    owners = facade_owner[0, :, 0]
    panels = facade_panel[0]
    panel_count = PAN_DEV
    terms = (
        jnp.zeros((groups * panel_count,), jnp.float32)
        .at[owners * panel_count + panels]
        .add(values)
    )
    force = lax.psum_scatter(terms, "space", scatter_dimension=0, tiled=True)
    return (moved[None], phi[None], force[None])


def solution(mesh):
    return jax.shard_map(
        body,
        mesh=mesh,
        in_specs=(
            P("dir", None, "space", None, None),
            P("dir", None, "space", None),
            P("dir", "space", None),
            P("dir", "space"),
            P("dir", "space", None),
            P("dir", "space"),
            P("dir", "space"),
        ),
        out_specs=(
            P("dir", None, "space", None, None),
            P("dir", "space", None, None),
            P("dir", "space"),
        ),
        check_vma=False,
    )
```

profile of v0, /device:TPU:264, one launch (start us, length us, event | category | flops | bytes accessed | tf_op | source)
XLA Modules:
  0.0 643.1 jit_solution(17695690492703726004)
XLA Ops:
  8.0 62.6 %psum.7 = f32[3,8,512]{2,1,0:T(8,128)} all-reduce(f32[3,8,512]{2,1,0:T(8,128)S(1)} %select_bitcast_fusion), channel_id=1, replica_groups=mesh['dir'=16,'space'=32] {'dir'}, use_global_device_ids=true, to_apply=%region_0.1 | all-reduce | flops 12288 | bytes 98304 | tf_op jit(solution)/shard_map/psum | solution.py:33
  72.7 80.0 %all-gather.2.cloned.1.call-done = f32[3,256,512]{2,1,0:T(8,128)} async-done(((f32[3,8,512]{2,1,0:T(8,128)}), f32[3,256,512]{2,1,0:T(8,128)}) %all-gather.2.cloned.1.call-update) | async-done | bytes 1572880 | tf_op jit(solution)/shard_map/all_gather | solution.py:101
  152.7 32.7 %copy.14 = f32[3,256,512]{0,2,1:T(8,128)} copy(f32[3,256,512]{2,1,0:T(8,128)} %all-gather.2.cloned.1.call-done) | data formatting | bytes 3145728 | tf_op jit(solution)/shard_map/all_gather | solution.py:101
  185.4 59.9 %gather_fusion = f32[4096,3]{1,0:T(8,128)} fusion(f32[3,131072]{0,1:T(8,128)} %bitcast.3, s32[4096]{0:T(1024)S(1)} %broadcast_clamp_fusion), kind=kCustom, calls=%fused_computation | custom fusion | bytes 114688 | tf_op jit(solution)/shard_map/jit(_take)/gather | solution.py:103
  245.4 2.3 copy.15
  248.5 2.1 collective-permute-start.2
  250.6 7.1 %collective-permute-start.3 = (f32[3,2,16,512]{3,2,1,0:T(8,128)S(1)}, f32[3,2,16,512]{3,2,1,0:T(8,128)S(1)}, u32[]{:S(2)}, u32[]{:S(2)}) collective-permute-start(f32[3,2,16,512]{3,2,1,0:T(8,128)S(1)} %get-tuple-element.85), channel_id=1, source_target_pairs={{1,0},{2,1},{3,2},{4,3},{5,4},{6,5},{7,6},{8,7},{9,8},{10,9},{11,1... | collective-permute-start | bytes 589832 | tf_op jit(solution)/shard_map/ppermute | solution.py:24
  259.2 1.7 collective-permute-done.3
  264.6 227.4 %while.14 = (s32[]{:T(128)}, f32[8,16,512]{2,1,0:T(8,128)S(1)}, f32[8,16,512]{2,1,0:T(8,128)S(1)}, s32[]{:T(128)}, s32[]{:T(128)}) while((s32[]{:T(128)}, f32[8,16,512]{2,1,0:T(8,128)S(1)}, f32[8,16,512]{2,1,0:T(8,128)S(1)}, s32[]{:T(128)}, s32[]{:T(128)}) %tuple.48), condition=%wide.region_2.3_spmd.clone, body=%wide.region_1.2_spmd.clone.sunk | while | flops 2108699 | bytes 3515959 | solution.py:119
  264.7 2.1 collective-permute-start
  266.7 7.3 %collective-permute-start.1 = (f32[1,16,512]{2,1,0:T(8,128)S(1)}, f32[1,16,512]{2,1,0:T(8,128)S(1)}, u32[]{:S(2)}, u32[]{:S(2)}) collective-permute-start(f32[1,16,512]{2,1,0:T(8,128)S(1)} %get-tuple-element.112), channel_id=1, source_target_pairs={{1,0},{2,1},{3,2},{4,3},{5,4},{6,5},{7,6},{8,7},{9,8},{10,9},{11,1... | collective-permute-start | bytes 98312 | tf_op jit(solution)/shard_map/while/body/eval_jaxpr/ppermute | solution.py:24
  274.0 1.6 collective-permute-done.1
  276.2 1.9 collective-permute-start
  278.1 7.3 %collective-permute-start.1 = (f32[1,16,512]{2,1,0:T(8,128)S(1)}, f32[1,16,512]{2,1,0:T(8,128)S(1)}, u32[]{:S(2)}, u32[]{:S(2)}) collective-permute-start(f32[1,16,512]{2,1,0:T(8,128)S(1)} %get-tuple-element.112), channel_id=1, source_target_pairs={{1,0},{2,1},{3,2},{4,3},{5,4},{6,5},{7,6},{8,7},{9,8},{10,9},{11,1... | collective-permute-start | bytes 98312 | tf_op jit(solution)/shard_map/while/body/eval_jaxpr/ppermute | solution.py:24
  285.4 1.6 collective-permute-done.1
  287.5 1.9 collective-permute-start
  289.5 7.3 %collective-permute-start.1 = (f32[1,16,512]{2,1,0:T(8,128)S(1)}, f32[1,16,512]{2,1,0:T(8,128)S(1)}, u32[]{:S(2)}, u32[]{:S(2)}) collective-permute-start(f32[1,16,512]{2,1,0:T(8,128)S(1)} %get-tuple-element.112), channel_id=1, source_target_pairs={{1,0},{2,1},{3,2},{4,3},{5,4},{6,5},{7,6},{8,7},{9,8},{10,9},{11,1... | collective-permute-start | bytes 98312 | tf_op jit(solution)/shard_map/while/body/eval_jaxpr/ppermute | solution.py:24
  296.8 1.6 collective-permute-done.1
  298.9 1.9 collective-permute-start
  300.8 7.3 %collective-permute-start.1 = (f32[1,16,512]{2,1,0:T(8,128)S(1)}, f32[1,16,512]{2,1,0:T(8,128)S(1)}, u32[]{:S(2)}, u32[]{:S(2)}) collective-permute-start(f32[1,16,512]{2,1,0:T(8,128)S(1)} %get-tuple-element.112), channel_id=1, source_target_pairs={{1,0},{2,1},{3,2},{4,3},{5,4},{6,5},{7,6},{8,7},{9,8},{10,9},{11,1... | collective-permute-start | bytes 98312 | tf_op jit(solution)/shard_map/while/body/eval_jaxpr/ppermute | solution.py:24
  308.1 1.6 collective-permute-done.1
  310.3 1.9 collective-permute-start
  312.2 7.3 %collective-permute-start.1 = (f32[1,16,512]{2,1,0:T(8,128)S(1)}, f32[1,16,512]{2,1,0:T(8,128)S(1)}, u32[]{:S(2)}, u32[]{:S(2)}) collective-permute-start(f32[1,16,512]{2,1,0:T(8,128)S(1)} %get-tuple-element.112), channel_id=1, source_target_pairs={{1,0},{2,1},{3,2},{4,3},{5,4},{6,5},{7,6},{8,7},{9,8},{10,9},{11,1... | collective-permute-start | bytes 98312 | tf_op jit(solution)/shard_map/while/body/eval_jaxpr/ppermute | solution.py:24
  319.5 1.6 collective-permute-done.1
  321.6 1.9 collective-permute-start
  323.6 7.3 %collective-permute-start.1 = (f32[1,16,512]{2,1,0:T(8,128)S(1)}, f32[1,16,512]{2,1,0:T(8,128)S(1)}, u32[]{:S(2)}, u32[]{:S(2)}) collective-permute-start(f32[1,16,512]{2,1,0:T(8,128)S(1)} %get-tuple-element.112), channel_id=1, source_target_pairs={{1,0},{2,1},{3,2},{4,3},{5,4},{6,5},{7,6},{8,7},{9,8},{10,9},{11,1... | collective-permute-start | bytes 98312 | tf_op jit(solution)/shard_map/while/body/eval_jaxpr/ppermute | solution.py:24
  330.8 1.6 collective-permute-done.1
  333.0 1.9 collective-permute-start
  334.9 7.3 %collective-permute-start.1 = (f32[1,16,512]{2,1,0:T(8,128)S(1)}, f32[1,16,512]{2,1,0:T(8,128)S(1)}, u32[]{:S(2)}, u32[]{:S(2)}) collective-permute-start(f32[1,16,512]{2,1,0:T(8,128)S(1)} %get-tuple-element.112), channel_id=1, source_target_pairs={{1,0},{2,1},{3,2},{4,3},{5,4},{6,5},{7,6},{8,7},{9,8},{10,9},{11,1... | collective-permute-start | bytes 98312 | tf_op jit(solution)/shard_map/while/body/eval_jaxpr/ppermute | solution.py:24
  342.2 1.6 collective-permute-done.1
  344.3 1.9 collective-permute-start
  346.3 7.3 %collective-permute-start.1 = (f32[1,16,512]{2,1,0:T(8,128)S(1)}, f32[1,16,512]{2,1,0:T(8,128)S(1)}, u32[]{:S(2)}, u32[]{:S(2)}) collective-permute-start(f32[1,16,512]{2,1,0:T(8,128)S(1)} %get-tuple-element.112), channel_id=1, source_target_pairs={{1,0},{2,1},{3,2},{4,3},{5,4},{6,5},{7,6},{8,7},{9,8},{10,9},{11,1... | collective-permute-start | bytes 98312 | tf_op jit(solution)/shard_map/while/body/eval_jaxpr/ppermute | solution.py:24
  353.6 1.6 collective-permute-done.1
  355.7 1.9 collective-permute-start
  357.6 7.3 %collective-permute-start.1 = (f32[1,16,512]{2,1,0:T(8,128)S(1)}, f32[1,16,512]{2,1,0:T(8,128)S(1)}, u32[]{:S(2)}, u32[]{:S(2)}) collective-permute-start(f32[1,16,512]{2,1,0:T(8,128)S(1)} %get-tuple-element.112), channel_id=1, source_target_pairs={{1,0},{2,1},{3,2},{4,3},{5,4},{6,5},{7,6},{8,7},{9,8},{10,9},{11,1... | collective-permute-start | bytes 98312 | tf_op jit(solution)/shard_map/while/body/eval_jaxpr/ppermute | solution.py:24
  364.9 1.6 collective-permute-done.1
  367.1 1.9 collective-permute-start
  369.0 7.3 %collective-permute-start.1 = (f32[1,16,512]{2,1,0:T(8,128)S(1)}, f32[1,16,512]{2,1,0:T(8,128)S(1)}, u32[]{:S(2)}, u32[]{:S(2)}) collective-permute-start(f32[1,16,512]{2,1,0:T(8,128)S(1)} %get-tuple-element.112), channel_id=1, source_target_pairs={{1,0},{2,1},{3,2},{4,3},{5,4},{6,5},{7,6},{8,7},{9,8},{10,9},{11,1... | collective-permute-start | bytes 98312 | tf_op jit(solution)/shard_map/while/body/eval_jaxpr/ppermute | solution.py:24
  376.3 1.6 collective-permute-done.1
  378.4 1.9 collective-permute-start
  380.4 7.3 %collective-permute-start.1 = (f32[1,16,512]{2,1,0:T(8,128)S(1)}, f32[1,16,512]{2,1,0:T(8,128)S(1)}, u32[]{:S(2)}, u32[]{:S(2)}) collective-permute-start(f32[1,16,512]{2,1,0:T(8,128)S(1)} %get-tuple-element.112), channel_id=1, source_target_pairs={{1,0},{2,1},{3,2},{4,3},{5,4},{6,5},{7,6},{8,7},{9,8},{10,9},{11,1... | collective-permute-start | bytes 98312 | tf_op jit(solution)/shard_map/while/body/eval_jaxpr/ppermute | solution.py:24
  389.8 1.9 collective-permute-start
  391.7 7.3 %collective-permute-start.1 = (f32[1,16,512]{2,1,0:T(8,128)S(1)}, f32[1,16,512]{2,1,0:T(8,128)S(1)}, u32[]{:S(2)}, u32[]{:S(2)}) collective-permute-start(f32[1,16,512]{2,1,0:T(8,128)S(1)} %get-tuple-element.112), channel_id=1, source_target_pairs={{1,0},{2,1},{3,2},{4,3},{5,4},{6,5},{7,6},{8,7},{9,8},{10,9},{11,1... | collective-permute-start | bytes 98312 | tf_op jit(solution)/shard_map/while/body/eval_jaxpr/ppermute | solution.py:24
  401.1 1.9 collective-permute-start
  403.1 7.3 %collective-permute-start.1 = (f32[1,16,512]{2,1,0:T(8,128)S(1)}, f32[1,16,512]{2,1,0:T(8,128)S(1)}, u32[]{:S(2)}, u32[]{:S(2)}) collective-permute-start(f32[1,16,512]{2,1,0:T(8,128)S(1)} %get-tuple-element.112), channel_id=1, source_target_pairs={{1,0},{2,1},{3,2},{4,3},{5,4},{6,5},{7,6},{8,7},{9,8},{10,9},{11,1... | collective-permute-start | bytes 98312 | tf_op jit(solution)/shard_map/while/body/eval_jaxpr/ppermute | solution.py:24
  412.5 1.9 collective-permute-start
  414.4 7.3 %collective-permute-start.1 = (f32[1,16,512]{2,1,0:T(8,128)S(1)}, f32[1,16,512]{2,1,0:T(8,128)S(1)}, u32[]{:S(2)}, u32[]{:S(2)}) collective-permute-start(f32[1,16,512]{2,1,0:T(8,128)S(1)} %get-tuple-element.112), channel_id=1, source_target_pairs={{1,0},{2,1},{3,2},{4,3},{5,4},{6,5},{7,6},{8,7},{9,8},{10,9},{11,1... | collective-permute-start | bytes 98312 | tf_op jit(solution)/shard_map/while/body/eval_jaxpr/ppermute | solution.py:24
  423.9 1.9 collective-permute-start
  425.8 7.3 %collective-permute-start.1 = (f32[1,16,512]{2,1,0:T(8,128)S(1)}, f32[1,16,512]{2,1,0:T(8,128)S(1)}, u32[]{:S(2)}, u32[]{:S(2)}) collective-permute-start(f32[1,16,512]{2,1,0:T(8,128)S(1)} %get-tuple-element.112), channel_id=1, source_target_pairs={{1,0},{2,1},{3,2},{4,3},{5,4},{6,5},{7,6},{8,7},{9,8},{10,9},{11,1... | collective-permute-start | bytes 98312 | tf_op jit(solution)/shard_map/while/body/eval_jaxpr/ppermute | solution.py:24
  435.2 1.9 collective-permute-start
  437.2 7.3 %collective-permute-start.1 = (f32[1,16,512]{2,1,0:T(8,128)S(1)}, f32[1,16,512]{2,1,0:T(8,128)S(1)}, u32[]{:S(2)}, u32[]{:S(2)}) collective-permute-start(f32[1,16,512]{2,1,0:T(8,128)S(1)} %get-tuple-element.112), channel_id=1, source_target_pairs={{1,0},{2,1},{3,2},{4,3},{5,4},{6,5},{7,6},{8,7},{9,8},{10,9},{11,1... | collective-permute-start | bytes 98312 | tf_op jit(solution)/shard_map/while/body/eval_jaxpr/ppermute | solution.py:24
  446.6 1.9 collective-permute-start
  448.5 7.3 %collective-permute-start.1 = (f32[1,16,512]{2,1,0:T(8,128)S(1)}, f32[1,16,512]{2,1,0:T(8,128)S(1)}, u32[]{:S(2)}, u32[]{:S(2)}) collective-permute-start(f32[1,16,512]{2,1,0:T(8,128)S(1)} %get-tuple-element.112), channel_id=1, source_target_pairs={{1,0},{2,1},{3,2},{4,3},{5,4},{6,5},{7,6},{8,7},{9,8},{10,9},{11,1... | collective-permute-start | bytes 98312 | tf_op jit(solution)/shard_map/while/body/eval_jaxpr/ppermute | solution.py:24
  457.9 1.9 collective-permute-start
  459.9 7.3 %collective-permute-start.1 = (f32[1,16,512]{2,1,0:T(8,128)S(1)}, f32[1,16,512]{2,1,0:T(8,128)S(1)}, u32[]{:S(2)}, u32[]{:S(2)}) collective-permute-start(f32[1,16,512]{2,1,0:T(8,128)S(1)} %get-tuple-element.112), channel_id=1, source_target_pairs={{1,0},{2,1},{3,2},{4,3},{5,4},{6,5},{7,6},{8,7},{9,8},{10,9},{11,1... | collective-permute-start | bytes 98312 | tf_op jit(solution)/shard_map/while/body/eval_jaxpr/ppermute | solution.py:24
  469.3 1.9 collective-permute-start
  471.2 7.3 %collective-permute-start.1 = (f32[1,16,512]{2,1,0:T(8,128)S(1)}, f32[1,16,512]{2,1,0:T(8,128)S(1)}, u32[]{:S(2)}, u32[]{:S(2)}) collective-permute-start(f32[1,16,512]{2,1,0:T(8,128)S(1)} %get-tuple-element.112), channel_id=1, source_target_pairs={{1,0},{2,1},{3,2},{4,3},{5,4},{6,5},{7,6},{8,7},{9,8},{10,9},{11,1... | collective-permute-start | bytes 98312 | tf_op jit(solution)/shard_map/while/body/eval_jaxpr/ppermute | solution.py:24
  480.7 1.9 collective-permute-start
  482.6 7.3 %collective-permute-start.1 = (f32[1,16,512]{2,1,0:T(8,128)S(1)}, f32[1,16,512]{2,1,0:T(8,128)S(1)}, u32[]{:S(2)}, u32[]{:S(2)}) collective-permute-start(f32[1,16,512]{2,1,0:T(8,128)S(1)} %get-tuple-element.112), channel_id=1, source_target_pairs={{1,0},{2,1},{3,2},{4,3},{5,4},{6,5},{7,6},{8,7},{9,8},{10,9},{11,1... | collective-permute-start | bytes 98312 | tf_op jit(solution)/shard_map/while/body/eval_jaxpr/ppermute | solution.py:24
  492.0 2.1 collective-permute-start.4
  494.1 7.3 %collective-permute-start.5 = (f32[1,16,512]{2,1,0:T(8,128)S(1)}, f32[1,16,512]{2,1,0:T(8,128)S(1)}, u32[]{:S(2)}, u32[]{:S(2)}) collective-permute-start(f32[1,16,512]{2,1,0:T(8,128)S(1)} %get-tuple-element.89), channel_id=1, source_target_pairs={{1,0},{2,1},{3,2},{4,3},{5,4},{6,5},{7,6},{8,7},{9,8},{10,9},{11,1... | collective-permute-start | bytes 98312 | tf_op jit(solution)/shard_map/ppermute | solution.py:24
  501.4 1.7 gather_fusion.1
  503.2 1.9 scatter_custom_fusion
  505.1 129.0 %all-reduce.4 = f32[4096]{0:T(1024)S(1)} all-reduce(f32[4096]{0:T(1024)S(1)} %scatter_custom_fusion), channel_id=2, replica_groups=mesh['dir'=16,'space'=32] {'space'}, use_global_device_ids=true, to_apply=%region_4.5.clone | all-reduce | flops 4096 | bytes 32768
  (161 shorter events, 36.8 us)
Async XLA Ops:
  7.2 0.8 copy-start.3
  7.2 63.4 %copy-start.2 = (s32[1,8,512]{2,1,0:T(8,128)S(1)}, s32[1,8,512]{2,1,0:T(8,128)}, u32[]{:S(2)}) copy-start(s32[1,8,512]{2,1,0:T(8,128)} %param.13) | copy-start | bytes 49156
  7.2 65.4 %copy-start.7 = (s32[1,256]{1,0:T(1,128)S(1)}, s32[1,256]{1,0:T(1,128)}, u32[]{:S(2)}) copy-start(s32[1,256]{1,0:T(1,128)} %param.14) | copy-start | bytes 3076
  7.2 145.5 %all-gather.2.cloned.1.call-start = ((), (), s32[]{:S(2)}) async-start(), calls=%async_computation | async-start | bytes 1622016 | tf_op jit(solution)/shard_map/all_gather | solution.py:101
  245.4 2.4 copy-start.1
  245.4 12.3 %copy-start.4 = (s32[1,256]{1,0:T(1,128)S(1)}, s32[1,256]{1,0:T(1,128)}, u32[]{:S(2)}) copy-start(s32[1,256]{1,0:T(1,128)} %param.16) | copy-start | bytes 3076
  245.4 12.3 %copy-start.5 = (s32[1,256,1]{1,2,0:T(1,128)S(1)}, s32[1,256,1]{1,2,0:T(1,128)}, u32[]{:S(2)}) copy-start(s32[1,256,1]{1,2,0:T(1,128)} %param.15) | copy-start | bytes 3076
  248.5 10.7 %collective-permute-start.2 = (f32[3,2,16,512]{3,2,1,0:T(8,128)S(1)}, f32[3,2,16,512]{3,2,1,0:T(8,128)S(1)}, u32[]{:S(2)}, u32[]{:S(2)}) collective-permute-start(f32[3,2,16,512]{3,2,1,0:T(8,128)S(1)} %get-tuple-element.84), channel_id=1, source_target_pairs={{0,1},{1,2},{2,3},{3,4},{4,5},{5,6},{6,7},{7,8},{8,9},{9,10},{10,1... | collective-permute-start | bytes 589832 | tf_op jit(solution)/shard_map/ppermute | solution.py:22
  250.6 10.2 %collective-permute-start.3 = (f32[3,2,16,512]{3,2,1,0:T(8,128)S(1)}, f32[3,2,16,512]{3,2,1,0:T(8,128)S(1)}, u32[]{:S(2)}, u32[]{:S(2)}) collective-permute-start(f32[3,2,16,512]{3,2,1,0:T(8,128)S(1)} %get-tuple-element.85), channel_id=1, source_target_pairs={{1,0},{2,1},{3,2},{4,3},{5,4},{6,5},{7,6},{8,7},{9,8},{10,9},{11,1... | collective-permute-start | bytes 589832 | tf_op jit(solution)/shard_map/ppermute | solution.py:24
  264.7 9.4 %collective-permute-start = (f32[1,16,512]{2,1,0:T(8,128)S(1)}, f32[1,16,512]{2,1,0:T(8,128)S(1)}, u32[]{:S(2)}, u32[]{:S(2)}) collective-permute-start(f32[1,16,512]{2,1,0:T(8,128)S(1)} %get-tuple-element.111), channel_id=1, source_target_pairs={{0,1},{1,2},{2,3},{3,4},{4,5},{5,6},{6,7},{7,8},{8,9},{9,10},{10,1... | collective-permute-start | bytes 98312 | tf_op jit(solution)/shard_map/while/body/eval_jaxpr/ppermute | solution.py:22
  266.7 8.9 %collective-permute-start.1 = (f32[1,16,512]{2,1,0:T(8,128)S(1)}, f32[1,16,512]{2,1,0:T(8,128)S(1)}, u32[]{:S(2)}, u32[]{:S(2)}) collective-permute-start(f32[1,16,512]{2,1,0:T(8,128)S(1)} %get-tuple-element.112), channel_id=1, source_target_pairs={{1,0},{2,1},{3,2},{4,3},{5,4},{6,5},{7,6},{8,7},{9,8},{10,9},{11,1... | collective-permute-start | bytes 98312 | tf_op jit(solution)/shard_map/while/body/eval_jaxpr/ppermute | solution.py:24
  276.2 9.2 %collective-permute-start = (f32[1,16,512]{2,1,0:T(8,128)S(1)}, f32[1,16,512]{2,1,0:T(8,128)S(1)}, u32[]{:S(2)}, u32[]{:S(2)}) collective-permute-start(f32[1,16,512]{2,1,0:T(8,128)S(1)} %get-tuple-element.111), channel_id=1, source_target_pairs={{0,1},{1,2},{2,3},{3,4},{4,5},{5,6},{6,7},{7,8},{8,9},{9,10},{10,1... | collective-permute-start | bytes 98312 | tf_op jit(solution)/shard_map/while/body/eval_jaxpr/ppermute | solution.py:22
  278.1 8.8 %collective-permute-start.1 = (f32[1,16,512]{2,1,0:T(8,128)S(1)}, f32[1,16,512]{2,1,0:T(8,128)S(1)}, u32[]{:S(2)}, u32[]{:S(2)}) collective-permute-start(f32[1,16,512]{2,1,0:T(8,128)S(1)} %get-tuple-element.112), channel_id=1, source_target_pairs={{1,0},{2,1},{3,2},{4,3},{5,4},{6,5},{7,6},{8,7},{9,8},{10,9},{11,1... | collective-permute-start | bytes 98312 | tf_op jit(solution)/shard_map/while/body/eval_jaxpr/ppermute | solution.py:24
  287.5 9.2 %collective-permute-start = (f32[1,16,512]{2,1,0:T(8,128)S(1)}, f32[1,16,512]{2,1,0:T(8,128)S(1)}, u32[]{:S(2)}, u32[]{:S(2)}) collective-permute-start(f32[1,16,512]{2,1,0:T(8,128)S(1)} %get-tuple-element.111), channel_id=1, source_target_pairs={{0,1},{1,2},{2,3},{3,4},{4,5},{5,6},{6,7},{7,8},{8,9},{9,10},{10,1... | collective-permute-start | bytes 98312 | tf_op jit(solution)/shard_map/while/body/eval_jaxpr/ppermute | solution.py:22
  289.5 8.8 %collective-permute-start.1 = (f32[1,16,512]{2,1,0:T(8,128)S(1)}, f32[1,16,512]{2,1,0:T(8,128)S(1)}, u32[]{:S(2)}, u32[]{:S(2)}) collective-permute-start(f32[1,16,512]{2,1,0:T(8,128)S(1)} %get-tuple-element.112), channel_id=1, source_target_pairs={{1,0},{2,1},{3,2},{4,3},{5,4},{6,5},{7,6},{8,7},{9,8},{10,9},{11,1... | collective-permute-start | bytes 98312 | tf_op jit(solution)/shard_map/while/body/eval_jaxpr/ppermute | solution.py:24
  298.9 9.2 %collective-permute-start = (f32[1,16,512]{2,1,0:T(8,128)S(1)}, f32[1,16,512]{2,1,0:T(8,128)S(1)}, u32[]{:S(2)}, u32[]{:S(2)}) collective-permute-start(f32[1,16,512]{2,1,0:T(8,128)S(1)} %get-tuple-element.111), channel_id=1, source_target_pairs={{0,1},{1,2},{2,3},{3,4},{4,5},{5,6},{6,7},{7,8},{8,9},{9,10},{10,1... | collective-permute-start | bytes 98312 | tf_op jit(solution)/shard_map/while/body/eval_jaxpr/ppermute | solution.py:22
  300.8 8.8 %collective-permute-start.1 = (f32[1,16,512]{2,1,0:T(8,128)S(1)}, f32[1,16,512]{2,1,0:T(8,128)S(1)}, u32[]{:S(2)}, u32[]{:S(2)}) collective-permute-start(f32[1,16,512]{2,1,0:T(8,128)S(1)} %get-tuple-element.112), channel_id=1, source_target_pairs={{1,0},{2,1},{3,2},{4,3},{5,4},{6,5},{7,6},{8,7},{9,8},{10,9},{11,1... | collective-permute-start | bytes 98312 | tf_op jit(solution)/shard_map/while/body/eval_jaxpr/ppermute | solution.py:24
  310.3 9.2 %collective-permute-start = (f32[1,16,512]{2,1,0:T(8,128)S(1)}, f32[1,16,512]{2,1,0:T(8,128)S(1)}, u32[]{:S(2)}, u32[]{:S(2)}) collective-permute-start(f32[1,16,512]{2,1,0:T(8,128)S(1)} %get-tuple-element.111), channel_id=1, source_target_pairs={{0,1},{1,2},{2,3},{3,4},{4,5},{5,6},{6,7},{7,8},{8,9},{9,10},{10,1... | collective-permute-start | bytes 98312 | tf_op jit(solution)/shard_map/while/body/eval_jaxpr/ppermute | solution.py:22
  312.2 8.8 %collective-permute-start.1 = (f32[1,16,512]{2,1,0:T(8,128)S(1)}, f32[1,16,512]{2,1,0:T(8,128)S(1)}, u32[]{:S(2)}, u32[]{:S(2)}) collective-permute-start(f32[1,16,512]{2,1,0:T(8,128)S(1)} %get-tuple-element.112), channel_id=1, source_target_pairs={{1,0},{2,1},{3,2},{4,3},{5,4},{6,5},{7,6},{8,7},{9,8},{10,9},{11,1... | collective-permute-start | bytes 98312 | tf_op jit(solution)/shard_map/while/body/eval_jaxpr/ppermute | solution.py:24
  321.6 9.2 %collective-permute-start = (f32[1,16,512]{2,1,0:T(8,128)S(1)}, f32[1,16,512]{2,1,0:T(8,128)S(1)}, u32[]{:S(2)}, u32[]{:S(2)}) collective-permute-start(f32[1,16,512]{2,1,0:T(8,128)S(1)} %get-tuple-element.111), channel_id=1, source_target_pairs={{0,1},{1,2},{2,3},{3,4},{4,5},{5,6},{6,7},{7,8},{8,9},{9,10},{10,1... | collective-permute-start | bytes 98312 | tf_op jit(solution)/shard_map/while/body/eval_jaxpr/ppermute | solution.py:22
  323.6 8.8 %collective-permute-start.1 = (f32[1,16,512]{2,1,0:T(8,128)S(1)}, f32[1,16,512]{2,1,0:T(8,128)S(1)}, u32[]{:S(2)}, u32[]{:S(2)}) collective-permute-start(f32[1,16,512]{2,1,0:T(8,128)S(1)} %get-tuple-element.112), channel_id=1, source_target_pairs={{1,0},{2,1},{3,2},{4,3},{5,4},{6,5},{7,6},{8,7},{9,8},{10,9},{11,1... | collective-permute-start | bytes 98312 | tf_op jit(solution)/shard_map/while/body/eval_jaxpr/ppermute | solution.py:24
  333.0 9.2 %collective-permute-start = (f32[1,16,512]{2,1,0:T(8,128)S(1)}, f32[1,16,512]{2,1,0:T(8,128)S(1)}, u32[]{:S(2)}, u32[]{:S(2)}) collective-permute-start(f32[1,16,512]{2,1,0:T(8,128)S(1)} %get-tuple-element.111), channel_id=1, source_target_pairs={{0,1},{1,2},{2,3},{3,4},{4,5},{5,6},{6,7},{7,8},{8,9},{9,10},{10,1... | collective-permute-start | bytes 98312 | tf_op jit(solution)/shard_map/while/body/eval_jaxpr/ppermute | solution.py:22
  334.9 8.8 %collective-permute-start.1 = (f32[1,16,512]{2,1,0:T(8,128)S(1)}, f32[1,16,512]{2,1,0:T(8,128)S(1)}, u32[]{:S(2)}, u32[]{:S(2)}) collective-permute-start(f32[1,16,512]{2,1,0:T(8,128)S(1)} %get-tuple-element.112), channel_id=1, source_target_pairs={{1,0},{2,1},{3,2},{4,3},{5,4},{6,5},{7,6},{8,7},{9,8},{10,9},{11,1... | collective-permute-start | bytes 98312 | tf_op jit(solution)/shard_map/while/body/eval_jaxpr/ppermute | solution.py:24
  344.3 9.2 %collective-permute-start = (f32[1,16,512]{2,1,0:T(8,128)S(1)}, f32[1,16,512]{2,1,0:T(8,128)S(1)}, u32[]{:S(2)}, u32[]{:S(2)}) collective-permute-start(f32[1,16,512]{2,1,0:T(8,128)S(1)} %get-tuple-element.111), channel_id=1, source_target_pairs={{0,1},{1,2},{2,3},{3,4},{4,5},{5,6},{6,7},{7,8},{8,9},{9,10},{10,1... | collective-permute-start | bytes 98312 | tf_op jit(solution)/shard_map/while/body/eval_jaxpr/ppermute | solution.py:22
  346.3 8.8 %collective-permute-start.1 = (f32[1,16,512]{2,1,0:T(8,128)S(1)}, f32[1,16,512]{2,1,0:T(8,128)S(1)}, u32[]{:S(2)}, u32[]{:S(2)}) collective-permute-start(f32[1,16,512]{2,1,0:T(8,128)S(1)} %get-tuple-element.112), channel_id=1, source_target_pairs={{1,0},{2,1},{3,2},{4,3},{5,4},{6,5},{7,6},{8,7},{9,8},{10,9},{11,1... | collective-permute-start | bytes 98312 | tf_op jit(solution)/shard_map/while/body/eval_jaxpr/ppermute | solution.py:24
  355.7 9.2 %collective-permute-start = (f32[1,16,512]{2,1,0:T(8,128)S(1)}, f32[1,16,512]{2,1,0:T(8,128)S(1)}, u32[]{:S(2)}, u32[]{:S(2)}) collective-permute-start(f32[1,16,512]{2,1,0:T(8,128)S(1)} %get-tuple-element.111), channel_id=1, source_target_pairs={{0,1},{1,2},{2,3},{3,4},{4,5},{5,6},{6,7},{7,8},{8,9},{9,10},{10,1... | collective-permute-start | bytes 98312 | tf_op jit(solution)/shard_map/while/body/eval_jaxpr/ppermute | solution.py:22
  357.6 8.8 %collective-permute-start.1 = (f32[1,16,512]{2,1,0:T(8,128)S(1)}, f32[1,16,512]{2,1,0:T(8,128)S(1)}, u32[]{:S(2)}, u32[]{:S(2)}) collective-permute-start(f32[1,16,512]{2,1,0:T(8,128)S(1)} %get-tuple-element.112), channel_id=1, source_target_pairs={{1,0},{2,1},{3,2},{4,3},{5,4},{6,5},{7,6},{8,7},{9,8},{10,9},{11,1... | collective-permute-start | bytes 98312 | tf_op jit(solution)/shard_map/while/body/eval_jaxpr/ppermute | solution.py:24
  367.1 9.2 %collective-permute-start = (f32[1,16,512]{2,1,0:T(8,128)S(1)}, f32[1,16,512]{2,1,0:T(8,128)S(1)}, u32[]{:S(2)}, u32[]{:S(2)}) collective-permute-start(f32[1,16,512]{2,1,0:T(8,128)S(1)} %get-tuple-element.111), channel_id=1, source_target_pairs={{0,1},{1,2},{2,3},{3,4},{4,5},{5,6},{6,7},{7,8},{8,9},{9,10},{10,1... | collective-permute-start | bytes 98312 | tf_op jit(solution)/shard_map/while/body/eval_jaxpr/ppermute | solution.py:22
  369.0 8.8 %collective-permute-start.1 = (f32[1,16,512]{2,1,0:T(8,128)S(1)}, f32[1,16,512]{2,1,0:T(8,128)S(1)}, u32[]{:S(2)}, u32[]{:S(2)}) collective-permute-start(f32[1,16,512]{2,1,0:T(8,128)S(1)} %get-tuple-element.112), channel_id=1, source_target_pairs={{1,0},{2,1},{3,2},{4,3},{5,4},{6,5},{7,6},{8,7},{9,8},{10,9},{11,1... | collective-permute-start | bytes 98312 | tf_op jit(solution)/shard_map/while/body/eval_jaxpr/ppermute | solution.py:24
  378.4 9.2 %collective-permute-start = (f32[1,16,512]{2,1,0:T(8,128)S(1)}, f32[1,16,512]{2,1,0:T(8,128)S(1)}, u32[]{:S(2)}, u32[]{:S(2)}) collective-permute-start(f32[1,16,512]{2,1,0:T(8,128)S(1)} %get-tuple-element.111), channel_id=1, source_target_pairs={{0,1},{1,2},{2,3},{3,4},{4,5},{5,6},{6,7},{7,8},{8,9},{9,10},{10,1... | collective-permute-start | bytes 98312 | tf_op jit(solution)/shard_map/while/body/eval_jaxpr/ppermute | solution.py:22
  380.4 8.8 %collective-permute-start.1 = (f32[1,16,512]{2,1,0:T(8,128)S(1)}, f32[1,16,512]{2,1,0:T(8,128)S(1)}, u32[]{:S(2)}, u32[]{:S(2)}) collective-permute-start(f32[1,16,512]{2,1,0:T(8,128)S(1)} %get-tuple-element.112), channel_id=1, source_target_pairs={{1,0},{2,1},{3,2},{4,3},{5,4},{6,5},{7,6},{8,7},{9,8},{10,9},{11,1... | collective-permute-start | bytes 98312 | tf_op jit(solution)/shard_map/while/body/eval_jaxpr/ppermute | solution.py:24
  389.8 9.2 %collective-permute-start = (f32[1,16,512]{2,1,0:T(8,128)S(1)}, f32[1,16,512]{2,1,0:T(8,128)S(1)}, u32[]{:S(2)}, u32[]{:S(2)}) collective-permute-start(f32[1,16,512]{2,1,0:T(8,128)S(1)} %get-tuple-element.111), channel_id=1, source_target_pairs={{0,1},{1,2},{2,3},{3,4},{4,5},{5,6},{6,7},{7,8},{8,9},{9,10},{10,1... | collective-permute-start | bytes 98312 | tf_op jit(solution)/shard_map/while/body/eval_jaxpr/ppermute | solution.py:22
  391.7 8.8 %collective-permute-start.1 = (f32[1,16,512]{2,1,0:T(8,128)S(1)}, f32[1,16,512]{2,1,0:T(8,128)S(1)}, u32[]{:S(2)}, u32[]{:S(2)}) collective-permute-start(f32[1,16,512]{2,1,0:T(8,128)S(1)} %get-tuple-element.112), channel_id=1, source_target_pairs={{1,0},{2,1},{3,2},{4,3},{5,4},{6,5},{7,6},{8,7},{9,8},{10,9},{11,1... | collective-permute-start | bytes 98312 | tf_op jit(solution)/shard_map/while/body/eval_jaxpr/ppermute | solution.py:24
  401.1 9.2 %collective-permute-start = (f32[1,16,512]{2,1,0:T(8,128)S(1)}, f32[1,16,512]{2,1,0:T(8,128)S(1)}, u32[]{:S(2)}, u32[]{:S(2)}) collective-permute-start(f32[1,16,512]{2,1,0:T(8,128)S(1)} %get-tuple-element.111), channel_id=1, source_target_pairs={{0,1},{1,2},{2,3},{3,4},{4,5},{5,6},{6,7},{7,8},{8,9},{9,10},{10,1... | collective-permute-start | bytes 98312 | tf_op jit(solution)/shard_map/while/body/eval_jaxpr/ppermute | solution.py:22
  403.1 8.8 %collective-permute-start.1 = (f32[1,16,512]{2,1,0:T(8,128)S(1)}, f32[1,16,512]{2,1,0:T(8,128)S(1)}, u32[]{:S(2)}, u32[]{:S(2)}) collective-permute-start(f32[1,16,512]{2,1,0:T(8,128)S(1)} %get-tuple-element.112), channel_id=1, source_target_pairs={{1,0},{2,1},{3,2},{4,3},{5,4},{6,5},{7,6},{8,7},{9,8},{10,9},{11,1... | collective-permute-start | bytes 98312 | tf_op jit(solution)/shard_map/while/body/eval_jaxpr/ppermute | solution.py:24
  412.5 9.2 %collective-permute-start = (f32[1,16,512]{2,1,0:T(8,128)S(1)}, f32[1,16,512]{2,1,0:T(8,128)S(1)}, u32[]{:S(2)}, u32[]{:S(2)}) collective-permute-start(f32[1,16,512]{2,1,0:T(8,128)S(1)} %get-tuple-element.111), channel_id=1, source_target_pairs={{0,1},{1,2},{2,3},{3,4},{4,5},{5,6},{6,7},{7,8},{8,9},{9,10},{10,1... | collective-permute-start | bytes 98312 | tf_op jit(solution)/shard_map/while/body/eval_jaxpr/ppermute | solution.py:22
  414.4 8.8 %collective-permute-start.1 = (f32[1,16,512]{2,1,0:T(8,128)S(1)}, f32[1,16,512]{2,1,0:T(8,128)S(1)}, u32[]{:S(2)}, u32[]{:S(2)}) collective-permute-start(f32[1,16,512]{2,1,0:T(8,128)S(1)} %get-tuple-element.112), channel_id=1, source_target_pairs={{1,0},{2,1},{3,2},{4,3},{5,4},{6,5},{7,6},{8,7},{9,8},{10,9},{11,1... | collective-permute-start | bytes 98312 | tf_op jit(solution)/shard_map/while/body/eval_jaxpr/ppermute | solution.py:24
  423.9 9.2 %collective-permute-start = (f32[1,16,512]{2,1,0:T(8,128)S(1)}, f32[1,16,512]{2,1,0:T(8,128)S(1)}, u32[]{:S(2)}, u32[]{:S(2)}) collective-permute-start(f32[1,16,512]{2,1,0:T(8,128)S(1)} %get-tuple-element.111), channel_id=1, source_target_pairs={{0,1},{1,2},{2,3},{3,4},{4,5},{5,6},{6,7},{7,8},{8,9},{9,10},{10,1... | collective-permute-start | bytes 98312 | tf_op jit(solution)/shard_map/while/body/eval_jaxpr/ppermute | solution.py:22
  425.8 8.8 %collective-permute-start.1 = (f32[1,16,512]{2,1,0:T(8,128)S(1)}, f32[1,16,512]{2,1,0:T(8,128)S(1)}, u32[]{:S(2)}, u32[]{:S(2)}) collective-permute-start(f32[1,16,512]{2,1,0:T(8,128)S(1)} %get-tuple-element.112), channel_id=1, source_target_pairs={{1,0},{2,1},{3,2},{4,3},{5,4},{6,5},{7,6},{8,7},{9,8},{10,9},{11,1... | collective-permute-start | bytes 98312 | tf_op jit(solution)/shard_map/while/body/eval_jaxpr/ppermute | solution.py:24
  435.2 9.2 %collective-permute-start = (f32[1,16,512]{2,1,0:T(8,128)S(1)}, f32[1,16,512]{2,1,0:T(8,128)S(1)}, u32[]{:S(2)}, u32[]{:S(2)}) collective-permute-start(f32[1,16,512]{2,1,0:T(8,128)S(1)} %get-tuple-element.111), channel_id=1, source_target_pairs={{0,1},{1,2},{2,3},{3,4},{4,5},{5,6},{6,7},{7,8},{8,9},{9,10},{10,1... | collective-permute-start | bytes 98312 | tf_op jit(solution)/shard_map/while/body/eval_jaxpr/ppermute | solution.py:22
  437.2 8.8 %collective-permute-start.1 = (f32[1,16,512]{2,1,0:T(8,128)S(1)}, f32[1,16,512]{2,1,0:T(8,128)S(1)}, u32[]{:S(2)}, u32[]{:S(2)}) collective-permute-start(f32[1,16,512]{2,1,0:T(8,128)S(1)} %get-tuple-element.112), channel_id=1, source_target_pairs={{1,0},{2,1},{3,2},{4,3},{5,4},{6,5},{7,6},{8,7},{9,8},{10,9},{11,1... | collective-permute-start | bytes 98312 | tf_op jit(solution)/shard_map/while/body/eval_jaxpr/ppermute | solution.py:24
  446.6 9.2 %collective-permute-start = (f32[1,16,512]{2,1,0:T(8,128)S(1)}, f32[1,16,512]{2,1,0:T(8,128)S(1)}, u32[]{:S(2)}, u32[]{:S(2)}) collective-permute-start(f32[1,16,512]{2,1,0:T(8,128)S(1)} %get-tuple-element.111), channel_id=1, source_target_pairs={{0,1},{1,2},{2,3},{3,4},{4,5},{5,6},{6,7},{7,8},{8,9},{9,10},{10,1... | collective-permute-start | bytes 98312 | tf_op jit(solution)/shard_map/while/body/eval_jaxpr/ppermute | solution.py:22
  448.5 8.8 %collective-permute-start.1 = (f32[1,16,512]{2,1,0:T(8,128)S(1)}, f32[1,16,512]{2,1,0:T(8,128)S(1)}, u32[]{:S(2)}, u32[]{:S(2)}) collective-permute-start(f32[1,16,512]{2,1,0:T(8,128)S(1)} %get-tuple-element.112), channel_id=1, source_target_pairs={{1,0},{2,1},{3,2},{4,3},{5,4},{6,5},{7,6},{8,7},{9,8},{10,9},{11,1... | collective-permute-start | bytes 98312 | tf_op jit(solution)/shard_map/while/body/eval_jaxpr/ppermute | solution.py:24
  457.9 9.2 %collective-permute-start = (f32[1,16,512]{2,1,0:T(8,128)S(1)}, f32[1,16,512]{2,1,0:T(8,128)S(1)}, u32[]{:S(2)}, u32[]{:S(2)}) collective-permute-start(f32[1,16,512]{2,1,0:T(8,128)S(1)} %get-tuple-element.111), channel_id=1, source_target_pairs={{0,1},{1,2},{2,3},{3,4},{4,5},{5,6},{6,7},{7,8},{8,9},{9,10},{10,1... | collective-permute-start | bytes 98312 | tf_op jit(solution)/shard_map/while/body/eval_jaxpr/ppermute | solution.py:22
  459.9 8.8 %collective-permute-start.1 = (f32[1,16,512]{2,1,0:T(8,128)S(1)}, f32[1,16,512]{2,1,0:T(8,128)S(1)}, u32[]{:S(2)}, u32[]{:S(2)}) collective-permute-start(f32[1,16,512]{2,1,0:T(8,128)S(1)} %get-tuple-element.112), channel_id=1, source_target_pairs={{1,0},{2,1},{3,2},{4,3},{5,4},{6,5},{7,6},{8,7},{9,8},{10,9},{11,1... | collective-permute-start | bytes 98312 | tf_op jit(solution)/shard_map/while/body/eval_jaxpr/ppermute | solution.py:24
  469.3 9.2 %collective-permute-start = (f32[1,16,512]{2,1,0:T(8,128)S(1)}, f32[1,16,512]{2,1,0:T(8,128)S(1)}, u32[]{:S(2)}, u32[]{:S(2)}) collective-permute-start(f32[1,16,512]{2,1,0:T(8,128)S(1)} %get-tuple-element.111), channel_id=1, source_target_pairs={{0,1},{1,2},{2,3},{3,4},{4,5},{5,6},{6,7},{7,8},{8,9},{9,10},{10,1... | collective-permute-start | bytes 98312 | tf_op jit(solution)/shard_map/while/body/eval_jaxpr/ppermute | solution.py:22
  471.2 8.8 %collective-permute-start.1 = (f32[1,16,512]{2,1,0:T(8,128)S(1)}, f32[1,16,512]{2,1,0:T(8,128)S(1)}, u32[]{:S(2)}, u32[]{:S(2)}) collective-permute-start(f32[1,16,512]{2,1,0:T(8,128)S(1)} %get-tuple-element.112), channel_id=1, source_target_pairs={{1,0},{2,1},{3,2},{4,3},{5,4},{6,5},{7,6},{8,7},{9,8},{10,9},{11,1... | collective-permute-start | bytes 98312 | tf_op jit(solution)/shard_map/while/body/eval_jaxpr/ppermute | solution.py:24
  480.7 9.2 %collective-permute-start = (f32[1,16,512]{2,1,0:T(8,128)S(1)}, f32[1,16,512]{2,1,0:T(8,128)S(1)}, u32[]{:S(2)}, u32[]{:S(2)}) collective-permute-start(f32[1,16,512]{2,1,0:T(8,128)S(1)} %get-tuple-element.111), channel_id=1, source_target_pairs={{0,1},{1,2},{2,3},{3,4},{4,5},{5,6},{6,7},{7,8},{8,9},{9,10},{10,1... | collective-permute-start | bytes 98312 | tf_op jit(solution)/shard_map/while/body/eval_jaxpr/ppermute | solution.py:22
  482.6 8.8 %collective-permute-start.1 = (f32[1,16,512]{2,1,0:T(8,128)S(1)}, f32[1,16,512]{2,1,0:T(8,128)S(1)}, u32[]{:S(2)}, u32[]{:S(2)}) collective-permute-start(f32[1,16,512]{2,1,0:T(8,128)S(1)} %get-tuple-element.112), channel_id=1, source_target_pairs={{1,0},{2,1},{3,2},{4,3},{5,4},{6,5},{7,6},{8,7},{9,8},{10,9},{11,1... | collective-permute-start | bytes 98312 | tf_op jit(solution)/shard_map/while/body/eval_jaxpr/ppermute | solution.py:24
  492.0 143.2 %copy-start = (f32[8,16,512]{2,1,0:T(8,128)}, f32[8,16,512]{2,1,0:T(8,128)S(1)}, u32[]{:S(2)}) copy-start(f32[8,16,512]{2,1,0:T(8,128)S(1)} %get-tuple-element.56) | copy-start | bytes 786436
  492.0 11.2 %copy-start.6 = (f32[1,256]{1,0:T(1,128)S(1)}, f32[1,256]{1,0:T(1,128)}, u32[]{:S(2)}) copy-start(f32[1,256]{1,0:T(1,128)} %param.17) | copy-start | bytes 3076
  492.0 142.7 %collective-permute-start.4 = (f32[1,16,512]{2,1,0:T(8,128)S(1)}, f32[1,16,512]{2,1,0:T(8,128)S(1)}, u32[]{:S(2)}, u32[]{:S(2)}) collective-permute-start(f32[1,16,512]{2,1,0:T(8,128)S(1)} %get-tuple-element.88), channel_id=1, source_target_pairs={{0,1},{1,2},{2,3},{3,4},{4,5},{5,6},{6,7},{7,8},{8,9},{9,10},{10,1... | collective-permute-start | bytes 98312 | tf_op jit(solution)/shard_map/ppermute | solution.py:22
  494.1 140.6 %collective-permute-start.5 = (f32[1,16,512]{2,1,0:T(8,128)S(1)}, f32[1,16,512]{2,1,0:T(8,128)S(1)}, u32[]{:S(2)}, u32[]{:S(2)}) collective-permute-start(f32[1,16,512]{2,1,0:T(8,128)S(1)} %get-tuple-element.89), channel_id=1, source_target_pairs={{1,0},{2,1},{3,2},{4,3},{5,4},{6,5},{7,6},{8,7},{9,8},{10,9},{11,1... | collective-permute-start | bytes 98312 | tf_op jit(solution)/shard_map/ppermute | solution.py:24
Sparse Core Ops, SparseCore 0:
  70.7 81.9 all-gather.1
where the time goes:
time: 646 us; the launch traced here: 643 us
  starting transfers between devices  202 us (31%)
  blocking collectives  192 us (30%)
  waiting for transfers between devices  115 us (18%)
  local copies, waits for them, and re-layouts  102 us (16%)
  other arithmetic  16.1 us (2%)
  between operations  15 us (2%)
    ppermute x22, starting transfers between devices, extended_2(): lax.ppermute(head, axis, [((i + 1) % count, i) for i in range(ends)])  160 us
    unnamed x1, blocking collectives  129 us
    all_gather x1, waiting for transfers between devices, body(): plane = lax.all_gather(plane_piece[0], 'space', axis=1, tiled=True)  80 us
    psum x1, blocking collectives, spread(): return lax.psum(block, axis)  62.6 us
    gather x2, local copies, waits for them, and re-layouts, body(): jnp.take(flat_plane, rot_map[0].reshape(-1), axis=1)  62.2 us
    ppermute x22, starting transfers between devices, extended_2(): lax.ppermute(tail, axis, [(i, (i + 1) % count) for i in range(ends)])  42.7 us
    ppermute x22, waiting for transfers between devices, extended_2(): lax.ppermute(head, axis, [((i + 1) % count, i) for i in range(ends)])  33 us
    all_gather x1, local copies, waits for them, and re-layouts, body(): plane = lax.all_gather(plane_piece[0], 'space', axis=1, tiled=True)  32.7 us
  transfers between devices with their start and end apart: 45, of which 23 were waited for; matrix products, arithmetic and copies ran while one was open for 1% of the time, Pallas kernels for 0%

commit v1 on v0

v1 whole, which is shorter than its diff:
```python
import math

import jax
import jax.numpy as jnp
import numpy as np
from jax import lax
from jax.experimental import pallas as pl
from jax.experimental.pallas import tpu as pltpu
from jax.sharding import PartitionSpec as P

ITERS = 20
PAN_DEV = 128
ROWS = 8
NX = 16
NZ = 512
NY = 256
GROUP = 32
LEVELS = 8
DIRS = 16
QUARTER = 128
TILES = 12
HALO = 20
WINDOW = 32 + 2 * HALO
FACADES = 256

time_step = 0.12
viscosity = 0.2

MESH = pl.DeviceIdType.MESH
EXACT = lax.Precision.HIGHEST


def sine_matrix(n):
    k = np.arange(1, n + 1)
    return np.sqrt(2.0 / (n + 1)) * np.sin(np.pi * np.outer(k, k) / (n + 1))


def sweep_taps():
    along_x = 2.0 * np.cos(np.pi * np.arange(1, NX + 1) / (NX + 1))
    along_z = 2.0 * np.cos(np.pi * np.arange(1, NZ + 1) / (NZ + 1))
    own = (along_x[:, None] + along_z[None, :]) / 36.0
    side = 16.0 / 36.0
    width = ITERS
    taps = np.zeros((2 * width + 1, NX, NZ))
    for _ in range(ITERS):
        moved = own * taps
        moved[1:] += side * taps[:-1]
        moved[:-1] += side * taps[1:]
        moved[width] -= 1.0 / 36.0
        taps = moved
    taps = taps[width : width + ITERS]
    return np.stack([taps[:, :, QUARTER * k : QUARTER * (k + 1)] for k in range(4)])


def remote(src, dst, send, recv, to):
    return pltpu.make_async_remote_copy(
        src_ref=src, dst_ref=dst, send_sem=send, recv_sem=recv, device_id=to, device_id_type=MESH
    )


def shift_lanes(q, by):
    lane = lax.broadcasted_iota(jnp.int32, q.shape, 1)
    if by == 1:
        return jnp.where(lane == NZ - 1, 0.0, pltpu.roll(q, NZ - 1, 1))
    return jnp.where(lane == 0, 0.0, pltpu.roll(q, 1, 1))


def shift_x(q, by, edge):
    row = lax.broadcasted_iota(jnp.int32, q.shape, 0)
    if by == 1:
        return jnp.where(row == NX - 1, edge(q), pltpu.roll(q, NX - 1, 0))
    return jnp.where(row == 0, edge(q), pltpu.roll(q, 1, 0))


def copied(q):
    return q


def empty(q):
    return 0.0


def dot(a, b):
    return lax.dot_general(a, b, (((1,), (0,)), ((), ())), precision=EXACT, preferred_element_type=jnp.float32)


def kernel(
    vel, prec, rot, fcell, fown, fpan, farea, sz_hbm, taps_hbm, kx, kx10,
    vout, pout, fout,
    uext, pb, rr, col, pbuf, infl, ust, sz, taps, xh, win, ph, bk, phi, fterm, frecv,
    selrow, colz, colp, cola, ohown,
    load_sem, s_u, r_u, s_p, r_p, s_r, r_r, s_t, r_t, s_i, r_i, s_x, r_x, s_b, r_b, s_f, r_f, l_p,
):
    d = lax.axis_index("dir")
    s = lax.axis_index("space")
    zc = s // 4
    j = s % 4
    chip = s // 2
    is_owner = (s % 2 == 0) & (chip % 4 != 3)
    my_tile = chip - chip // 4
    owners = [2 * (t + t // 3) for t in range(TILES)]

    load_u = pltpu.make_async_copy(vel.at[0], uext.at[:, pl.ds(2, ROWS)], load_sem.at[0])
    load_u.start()
    load_s = pltpu.make_async_copy(sz_hbm, sz, load_sem.at[1])
    load_s.start()
    load_t = pltpu.make_async_copy(taps_hbm.at[j], taps, load_sem.at[2])
    load_t.start()

    barrier = pltpu.get_barrier_semaphore()
    for k in range(1, GROUP):
        pl.semaphore_signal(barrier, inc=1, device_id=(d, (s + k) % GROUP), device_id_type=MESH)

    @pl.when(d != 0)
    def _():
        pl.semaphore_signal(barrier, inc=1, device_id=(0, s), device_id_type=MESH)
        pl.semaphore_wait(barrier, GROUP - 1)

    @pl.when(d == 0)
    def _():
        pl.semaphore_wait(barrier, GROUP - 1 + DIRS - 1)

    @pl.when(d == 0)
    def _():
        for k in range(1, DIRS):
            remote(prec.at[0], pb, s_p.at[k], r_p, (k, s)).start()

    for t in range(TILES):
        @pl.when(s != owners[t])
        def _(t=t):
            remote(rot.at[0, :, pl.ds(0, 128)], rr.at[pl.ds(8 * s, 8)], s_r, r_r, (d, owners[t])).start()

    up = (d, (s + 1) % GROUP)
    down = (d, (s + GROUP - 1) % GROUP)
    edges = [
        remote(vel.at[0, :, pl.ds(7, 1)], uext.at[:, pl.ds(1, 1)], s_u.at[0], r_u.at[0], up),
        remote(vel.at[0, pl.ds(1, 1), pl.ds(6, 1)], uext.at[pl.ds(1, 1), pl.ds(0, 1)], s_u.at[1], r_u.at[1], up),
        remote(vel.at[0, :, pl.ds(0, 1)], uext.at[:, pl.ds(10, 1)], s_u.at[2], r_u.at[2], down),
        remote(vel.at[0, pl.ds(1, 1), pl.ds(1, 1)], uext.at[pl.ds(1, 1), pl.ds(11, 1)], s_u.at[3], r_u.at[3], down),
    ]
    for edge in edges:
        edge.start()

    def column(row):
        return jnp.transpose(jnp.broadcast_to(row, (128, FACADES)))

    cell = column(fcell[...])
    lane = lax.broadcasted_iota(jnp.int32, (FACADES, 128), 1)
    selrow[...] = jnp.where((cell >> 9) == lane, 1.0, 0.0)
    colz[...] = cell & 511
    colp[...] = column(fpan[...])
    cola[...] = column(farea[...])
    ohown[...] = jnp.where(
        lax.broadcasted_iota(jnp.int32, (GROUP, FACADES), 0) == jnp.broadcast_to(fown[...], (GROUP, FACADES)), 1.0, 0.0
    )

    @pl.when(d == 0)
    def _():
        own = pltpu.make_async_copy(prec.at[0], pb, l_p)
        own.start()
        own.wait()

    @pl.when(d != 0)
    def _():
        remote(prec.at[0], pb, s_p.at[0], r_p, (0, s)).wait_recv()

    for t in range(TILES):
        c, k = t // 4, t % 4

        @pl.when(s != owners[t])
        def _(t=t, c=c, k=k):
            remote(pb.at[c, :, pl.ds(128 * k, 128)], col.at[pl.ds(8 * s, 8)], s_t, r_t, (d, owners[t])).start()

        @pl.when(s == owners[t])
        def _(t=t, c=c, k=k):
            col[pl.ds(pl.multiple_of(8 * s, 8), 8), :] = pb[c, :, 128 * k : 128 * (k + 1)]
            rr[pl.ds(pl.multiple_of(8 * s, 8), 8), :] = rot[0, :, 0:128]

    @pl.when(is_owner)
    def _():
        part = pl.ds(0, 8 * (GROUP - 1))
        remote(rr.at[part], rr.at[part], s_r, r_r, (d, (s + 1) % GROUP)).wait_recv()
        q = rr[...] >> 9
        lane = lax.broadcasted_iota(jnp.int32, (NY, 128), 1)
        low = jnp.where(q == lane, 1.0, 0.0)
        high = jnp.where(q - 128 == lane, 1.0, 0.0)
        pbuf[0:8, :] = jnp.zeros((8, 128), jnp.float32)
        pbuf[NY : NY + 8, :] = jnp.zeros((8, 128), jnp.float32)
        remote(col.at[part], col.at[part], s_t, r_t, (d, (s + 1) % GROUP)).wait_recv()
        pbuf[4 : NY + 4, :] = dot(low, col[0:128, :]) + dot(high, col[128:256, :])

        def send(k, carry):
            to = (s + k) % GROUP
            remote(pbuf.at[pl.ds(8 * to, 16)], infl.at[my_tile], s_i, r_i, (d, to)).start()
            return carry

        lax.fori_loop(1, GROUP, send, 0)
        infl[my_tile] = pbuf[pl.ds(pl.multiple_of(8 * s, 8), 16), :]

    load_u.wait()
    for edge in edges:
        edge.wait()

    @pl.when(is_owner)
    def _():
        part = pl.ds(0, TILES - 1)
        remote(infl.at[part], infl.at[part], s_i, r_i, (d, (s + 1) % GROUP)).wait_recv()

    @pl.when(jnp.logical_not(is_owner))
    def _():
        remote(infl, infl, s_i, r_i, (d, (s + 1) % GROUP)).wait_recv()

    for t in range(TILES):
        c, k = t // 4, t % 4
        for r in range(ROWS + 4):
            uext[c, r, 0:1, 128 * k : 128 * (k + 1)] = infl[t, r + 2 : r + 3, :]

    blank = jnp.zeros((2, NX, NZ), jnp.float32)

    @pl.when(s == 0)
    def _():
        for c in range(3):
            uext[c, 0:2] = blank

    @pl.when(s == GROUP - 1)
    def _():
        for c in range(3):
            uext[c, 10:12] = blank

    def tentative(c, r):
        q = uext[c, r]
        yplus = uext[c, r + 1]
        yminus = uext[c, r - 1]
        xplus, xminus = shift_x(q, 1, copied), shift_x(q, -1, copied)
        zplus, zminus = shift_lanes(q, 1), shift_lanes(q, -1)
        lap = xplus + xminus + zplus + zminus + 16.0 * (yplus + yminus) - 36.0 * q
        advect = (
            uext[0, r] * (xplus - xminus) * 0.5
            + uext[1, r] * (yplus - yminus) * 2.0
            + uext[2, r] * (zplus - zminus) * 0.5
        )
        ust[c, r - 1] = q + time_step * (viscosity * lap - advect)

    def row_y(r, carry):
        tentative(1, r)
        return carry

    def row_xz(r, carry):
        tentative(0, r)
        tentative(2, r)
        return carry

    lax.fori_loop(1, ROWS + 3, row_y, 0)
    lax.fori_loop(2, ROWS + 2, row_xz, 0)

    @pl.when(s == 0)
    def _():
        ust[1, 0] = jnp.zeros((NX, NZ), jnp.float32)

    @pl.when(s == GROUP - 1)
    def _():
        ust[1, ROWS + 1] = jnp.zeros((NX, NZ), jnp.float32)

    def row_div(r, carry):
        qx = ust[0, r + 1]
        qz = ust[2, r + 1]
        along_x = (shift_x(qx, 1, copied) - shift_x(qx, -1, copied)) * 0.5
        along_y = (ust[1, r + 2] - ust[1, r]) * 2.0
        along_z = (shift_lanes(qz, 1) - shift_lanes(qz, -1)) * 0.5
        phi[r] = along_x + along_y + along_z
        return carry

    lax.fori_loop(0, ROWS, row_div, 0)

    load_s.wait()
    modes = dot(dot(kx[...], phi[0:ROWS].reshape(ROWS * NX, NZ)), sz[...])
    for k in range(4):
        xh[k] = modes[:, 128 * k : 128 * (k + 1)].reshape(ROWS, NX, QUARTER)

    for dk in range(1, 4):
        k = (j + dk) % 4
        remote(xh.at[k], win.at[pl.ds(HALO + 8 * j, 8)], s_x, r_x, (d, 4 * zc + k)).start()
    above = 4 * ((zc + 1) % LEVELS)
    below = 4 * ((zc + LEVELS - 1) % LEVELS)

    @pl.when(j >= 2)
    def _():
        for k in range(4):
            remote(xh.at[k], win.at[pl.ds(8 * j - 12, 8)], s_x, r_x, (d, above + k)).start()

    @pl.when(j == 1)
    def _():
        for k in range(4):
            remote(xh.at[k, pl.ds(4, 4)], win.at[pl.ds(0, 4)], s_x, r_x, (d, above + k)).start()

    @pl.when(j <= 1)
    def _():
        for k in range(4):
            remote(xh.at[k], win.at[pl.ds(HALO + 32 + 8 * j, 8)], s_x, r_x, (d, below + k)).start()

    @pl.when(j == 2)
    def _():
        for k in range(4):
            remote(xh.at[k, pl.ds(0, 4)], win.at[pl.ds(WINDOW - 4, 4)], s_x, r_x, (d, below + k)).start()

    win[pl.ds(HALO + 8 * j, 8)] = xh[j]
    load_t.wait()
    others = pl.ds(0, WINDOW - 8)
    remote(win.at[others], win.at[others], s_x, r_x, (d, (s + 1) % GROUP)).wait_recv()

    @pl.when(zc == 0)
    def _():
        win[HALO - 1] = jnp.zeros((NX, QUARTER), jnp.float32)
        for i in range(1, HALO):
            win[HALO - 1 - i] = -win[HALO - 1 + i]

    @pl.when(zc == LEVELS - 1)
    def _():
        win[HALO + 32] = jnp.zeros((NX, QUARTER), jnp.float32)
        for i in range(1, HALO):
            win[HALO + 32 + i] = -win[HALO + 32 - i]

    def filter_row(y, carry):
        total = taps[0] * win[y + 19]
        for i in range(1, ITERS):
            total = total + taps[i] * (win[y + 19 + i] + win[y + 19 - i])
        ph[y] = total
        return carry

    lax.fori_loop(0, 34, filter_row, 0)

    for dk in range(1, 4):
        k = (j + dk) % 4
        remote(ph.at[pl.ds(8 * k, 10)], bk.at[j], s_b, r_b, (d, 4 * zc + k)).start()
    bk[j] = ph[pl.ds(8 * j, 10)]
    back = pl.ds(0, 3)
    remote(bk.at[back], bk.at[back], s_b, r_b, (d, (s + 1) % GROUP)).wait_recv()

    spread = sum(dot(bk[k].reshape(10 * NX, QUARTER), sz[128 * k : 128 * (k + 1), :]) for k in range(4))
    phi[...] = dot(kx10[...], spread).reshape(10, NX, NZ)

    @pl.when(s == 0)
    def _():
        phi[0] = jnp.zeros((NX, NZ), jnp.float32)

    @pl.when(s == GROUP - 1)
    def _():
        phi[ROWS + 1] = jnp.zeros((NX, NZ), jnp.float32)

    lines = dot(selrow[...], phi[1 : ROWS + 1].reshape(ROWS * NX, NZ))
    zlane = lax.broadcasted_iota(jnp.int32, (FACADES, NZ), 1)
    value = jnp.sum(jnp.where(colz[:, 0:1] == zlane, lines, 0.0), axis=1, keepdims=True) * cola[:, 0:1]
    lane = lax.broadcasted_iota(jnp.int32, (FACADES, 128), 1)
    terms = dot(ohown[...], jnp.where(colp[...] == lane, value, 0.0))
    for o in range(GROUP):
        fterm[o] = terms[o : o + 1, :]

    def send_terms(k, carry):
        to = (s + k) % GROUP
        remote(fterm.at[to], frecv.at[s], s_f, r_f, (d, to)).start()
        return carry

    lax.fori_loop(1, GROUP, send_terms, 0)
    frecv[s] = fterm[s]

    def row_out(r, carry):
        q = phi[r + 1]
        vout[0, 0, r] = ust[0, r + 1] - (shift_x(q, 1, empty) - shift_x(q, -1, empty)) * 0.5
        vout[0, 1, r] = ust[1, r + 1] - (phi[r + 2] - phi[r]) * 2.0
        vout[0, 2, r] = ust[2, r + 1] - (shift_lanes(q, 1) - shift_lanes(q, -1)) * 0.5
        pout[0, r] = q
        return carry

    lax.fori_loop(0, ROWS, row_out, 0)

    @pl.when(d == 0)
    def _():
        for k in range(1, DIRS):
            remote(prec.at[0], pb, s_p.at[k], r_p, (k, s)).wait_send()

    eight = pl.ds(0, 8 * (TILES - 1))

    remote(rr.at[eight], rr.at[eight], s_r, r_r, up).wait_send()
    remote(col.at[eight], col.at[eight], s_t, r_t, up).wait_send()

    @pl.when(jnp.logical_not(is_owner))
    def _():
        remote(rr.at[pl.ds(0, 8)], rr.at[pl.ds(0, 8)], s_r, r_r, up).wait_send()
        remote(col.at[pl.ds(0, 8)], col.at[pl.ds(0, 8)], s_t, r_t, up).wait_send()

    @pl.when(is_owner)
    def _():
        sent = pl.ds(0, GROUP - 1)
        remote(win.at[sent], win.at[sent], s_i, r_i, up).wait_send()

    @pl.when((j == 0) | (j == 3))
    def _():
        remote(win.at[pl.ds(0, 56)], win.at[pl.ds(0, 56)], s_x, r_x, up).wait_send()

    @pl.when((j == 1) | (j == 2))
    def _():
        remote(win, win, s_x, r_x, up).wait_send()

    remote(bk.at[back], bk.at[back], s_b, r_b, up).wait_send()
    rest = pl.ds(0, GROUP - 1)
    remote(frecv.at[rest], frecv.at[rest], s_f, r_f, up).wait()
    fout[...] = jnp.sum(frecv[...], axis=0)


def body(velocity, precursor, rot_map, facade_cell, facade_owner, facade_panel, facade_area):
    f32 = jnp.float32
    across = sine_matrix(NX)
    constants = [
        jnp.asarray(sine_matrix(NZ), f32),
        jnp.asarray(sweep_taps(), f32),
        jnp.asarray(np.kron(np.eye(ROWS), across), f32),
        jnp.asarray(np.kron(np.eye(ROWS + 2), across), f32),
    ]
    far = pl.BlockSpec(memory_space=pl.ANY)
    near = pl.BlockSpec(memory_space=pltpu.VMEM)
    dma = pltpu.SemaphoreType.DMA
    return pl.pallas_call(
        kernel,
        out_shape=(
            jax.ShapeDtypeStruct((1, 3, ROWS, NX, NZ), f32),
            jax.ShapeDtypeStruct((1, ROWS, NX, NZ), f32),
            jax.ShapeDtypeStruct((1, PAN_DEV), f32),
        ),
        in_specs=[far, far, near, near, near, near, near, far, far, near, near],
        out_specs=(near, near, near),
        scratch_shapes=[
            pltpu.VMEM((3, ROWS + 4, NX, NZ), f32),
            pltpu.VMEM((3, ROWS, NZ), f32),
            pltpu.VMEM((NY, 128), jnp.int32),
            pltpu.VMEM((NY, 128), f32),
            pltpu.VMEM((NY + 8, 128), f32),
            pltpu.VMEM((TILES, 16, 128), f32),
            pltpu.VMEM((3, ROWS + 2, NX, NZ), f32),
            pltpu.VMEM((NZ, NZ), f32),
            pltpu.VMEM((ITERS, NX, QUARTER), f32),
            pltpu.VMEM((4, ROWS, NX, QUARTER), f32),
            pltpu.VMEM((WINDOW, NX, QUARTER), f32),
            pltpu.VMEM((34, NX, QUARTER), f32),
            pltpu.VMEM((4, ROWS + 2, NX, QUARTER), f32),
            pltpu.VMEM((ROWS + 2, NX, NZ), f32),
            pltpu.VMEM((GROUP, 1, PAN_DEV), f32),
            pltpu.VMEM((GROUP, 1, PAN_DEV), f32),
            pltpu.VMEM((FACADES, 128), f32),
            pltpu.VMEM((FACADES, 128), jnp.int32),
            pltpu.VMEM((FACADES, 128), jnp.int32),
            pltpu.VMEM((FACADES, 128), f32),
            pltpu.VMEM((GROUP, FACADES), f32),
            dma((3,)), dma((4,)), dma((4,)), dma((DIRS,)),
            dma, dma, dma, dma, dma, dma, dma, dma, dma, dma, dma, dma, dma, dma,
        ],
        compiler_params=pltpu.CompilerParams(
            collective_id=0, has_side_effects=True, vmem_limit_bytes=48 << 20
        ),
    )(
        velocity, precursor, rot_map, facade_cell, facade_owner.reshape(1, FACADES), facade_panel, facade_area, *constants
    )


def solution(mesh):
    return jax.shard_map(
        body,
        mesh=mesh,
        in_specs=(
            P("dir", None, "space", None, None),
            P("dir", None, "space", None),
            P("dir", "space", None),
            P("dir", "space"),
            P("dir", "space", None),
            P("dir", "space"),
            P("dir", "space"),
        ),
        out_specs=(
            P("dir", None, "space", None, None),
            P("dir", "space", None, None),
            P("dir", "space"),
        ),
        check_vma=False,
    )
```

time: 646 us -> 78.8 us (0.12)
  the two profiles are of different devices: /device:TPU:264 before, /device:TPU:33 now
where the time goes in v1:
time: 78.8 us; the launch traced here: 78.3 us
  Pallas kernels  66.1 us (84%)
  local copies, waits for them, and re-layouts  11.5 us (15%)
    pallas_call x1, Pallas kernels, body(): pl.pallas_call(kernel, out_shape=(jax.ShapeDtypeStruct((1, 3, ROWS, NX, N...  66.1 us
    unnamed x25, local copies, waits for them, and re-layouts  11.5 us

profile of v1, /device:TPU:33, one launch (start us, length us, event | category | flops | bytes accessed | tf_op | source)
XLA Modules:
  0.0 78.3 jit_solution(4453393922542416985)
XLA Ops:
  0.6 0.0 copy-start.7
  0.6 0.7 copy-done.7
  1.3 0.0 copy-start
  1.3 1.2 %copy-done = f32[512,512]{1,0:T(8,128)S(1)} copy-done((f32[512,512]{1,0:T(8,128)S(1)}, f32[512,512]{1,0:T(8,128)}, u32[]{:S(2)}) %copy-start) | copy-done | bytes 1048600
  2.5 0.0 copy-start.1
  2.5 1.1 %copy-done.1 = f32[1,3,8,16,512]{4,3,2,1,0:T(8,128)S(1)} copy-done((f32[1,3,8,16,512]{4,3,2,1,0:T(8,128)S(1)}, f32[1,3,8,16,512]{4,3,2,1,0:T(8,128)}, u32[]{:S(2)}) %copy-start.1) | copy-done | bytes 786456
  3.7 0.0 copy-start.2
  3.7 1.1 %copy-done.2 = f32[4,20,16,128]{3,2,1,0:T(8,128)S(1)} copy-done((f32[4,20,16,128]{3,2,1,0:T(8,128)S(1)}, f32[4,20,16,128]{3,2,1,0:T(8,128)}, u32[]{:S(2)}) %copy-start.2) | copy-done | bytes 655384
  4.8 0.0 copy-start.3
  4.8 0.9 %copy-done.3 = f32[160,160]{1,0:T(8,128)S(1)} copy-done((f32[160,160]{1,0:T(8,128)S(1)}, f32[160,160]{1,0:T(8,128)}, u32[]{:S(2)}) %copy-start.3) | copy-done | bytes 102424
  5.7 0.0 copy-start.4
  5.7 0.8 %copy-done.4 = f32[128,128]{1,0:T(8,128)S(1)} copy-done((f32[128,128]{1,0:T(8,128)S(1)}, f32[128,128]{1,0:T(8,128)}, u32[]{:S(2)}) %copy-start.4) | copy-done | bytes 65560
  6.5 0.0 copy-start.5
  6.5 0.8 %copy-done.5 = f32[1,3,8,512]{3,2,1,0:T(8,128)S(1)} copy-done((f32[1,3,8,512]{3,2,1,0:T(8,128)S(1)}, f32[1,3,8,512]{3,2,1,0:T(8,128)}, u32[]{:S(2)}) %copy-start.5) | copy-done | bytes 49176
  7.3 0.0 copy-start.6
  7.3 0.7 copy-done.6
  8.0 0.0 copy-start.8
  8.0 0.7 copy-done.8
  8.7 0.0 copy-start.9
  8.7 0.7 copy-done.9
  9.4 0.0 copy-start.10
  9.4 0.7 copy-done.10
  10.1 66.1 %shard_map.130 = (f32[1,3,8,16,512]{4,3,2,1,0:T(8,128)S(1)}, f32[1,8,16,512]{3,2,1,0:T(8,128)S(1)}, f32[1,128]{1,0:T(1,128)S(1)}) custom-call(f32[1,3,8,16,512]{4,3,2,1,0:T(8,128)S(1)} %copy-done.1, f32[1,3,8,512]{3,2,1,0:T(8,128)S(1)} %copy-done.5, s32[1,8,512]{2,1,0:T(8,128)S(1)} %copy-done.6, s32[1,256]{1,0:T(1,128)S(1)} %copy-done.7, ...), custom_call_target="tpu_custom_call" | custom-call | tf_op jit(solution)/shard_map/pallas_call | solution.py:422
  76.2 0.9 %copy.17 = f32[1,3,8,16,512]{4,3,2,1,0:T(8,128)} copy(f32[1,3,8,16,512]{4,3,2,1,0:T(8,128)S(1)} %get-tuple-element.6) | data formatting | bytes 1572864
  77.1 0.7 copy.18
  77.8 0.5 copy.19
Async XLA Ops:
  0.6 0.7 copy-start.7
  1.3 1.2 %copy-start = (f32[512,512]{1,0:T(8,128)S(1)}, f32[512,512]{1,0:T(8,128)}, u32[]{:S(2)}) copy-start(f32[512,512]{1,0:T(8,128)} %constant.8.clone.sz_hbm) | copy-start | bytes 3145732
  2.5 1.1 %copy-start.1 = (f32[1,3,8,16,512]{4,3,2,1,0:T(8,128)S(1)}, f32[1,3,8,16,512]{4,3,2,1,0:T(8,128)}, u32[]{:S(2)}) copy-start(f32[1,3,8,16,512]{4,3,2,1,0:T(8,128)} %vel.1) | copy-start | bytes 2359300
  3.7 1.1 %copy-start.2 = (f32[4,20,16,128]{3,2,1,0:T(8,128)S(1)}, f32[4,20,16,128]{3,2,1,0:T(8,128)}, u32[]{:S(2)}) copy-start(f32[4,20,16,128]{3,2,1,0:T(8,128)} %constant.9.clone.taps_hbm) | copy-start | bytes 1966084
  4.8 0.9 %copy-start.3 = (f32[160,160]{1,0:T(8,128)S(1)}, f32[160,160]{1,0:T(8,128)}, u32[]{:S(2)}) copy-start(f32[160,160]{1,0:T(8,128)} %constant.11.clone.kx10) | copy-start | bytes 307204
  5.7 0.8 %copy-start.4 = (f32[128,128]{1,0:T(8,128)S(1)}, f32[128,128]{1,0:T(8,128)}, u32[]{:S(2)}) copy-start(f32[128,128]{1,0:T(8,128)} %constant.10.clone.kx) | copy-start | bytes 196612
  6.5 0.8 %copy-start.5 = (f32[1,3,8,512]{3,2,1,0:T(8,128)S(1)}, f32[1,3,8,512]{3,2,1,0:T(8,128)}, u32[]{:S(2)}) copy-start(f32[1,3,8,512]{3,2,1,0:T(8,128)} %prec.1) | copy-start | bytes 147460
  7.3 0.7 copy-start.6
  8.0 0.7 copy-start.8
  8.7 0.7 copy-start.9
  9.4 0.7 copy-start.10

commit v2 on v1

--- a/solution.py
+++ b/solution.py
@@ -19,7 +19,8 @@
 DIRS = 16
 QUARTER = 128
 TILES = 12
-HALO = 20
+HALO = 24
+LATE = 3
 WINDOW = 32 + 2 * HALO
 FACADES = 256
 
@@ -85,11 +86,13 @@
 
 
 def kernel(
-    vel, prec, rot, fcell, fown, fpan, farea, sz_hbm, taps_hbm, kx, kx10,
+    vel, prec, rot, fcell_hbm, fown_hbm, fpan_hbm, farea_hbm, sz_hbm, taps_hbm, kx_hbm, kx10_hbm, sx_hbm,
     vout, pout, fout,
+    fcell, fown, fpan, farea, kx, kx10, sx,
+    near_x, inlet, xl, wl,
     uext, pb, rr, col, pbuf, infl, ust, sz, taps, xh, win, ph, bk, phi, fterm, frecv,
     selrow, colz, colp, cola, ohown,
-    load_sem, s_u, r_u, s_p, r_p, s_r, r_r, s_t, r_t, s_i, r_i, s_x, r_x, s_b, r_b, s_f, r_f, l_p,
+    load_sem, go, s_u, r_u, s_p, r_p, s_r, r_r, s_t, r_t, s_i, r_i, s_x, r_x, s_l, r_l, s_b, r_b, s_f, r_f, l_p,
 ):
     d = lax.axis_index("dir")
     s = lax.axis_index("space")
@@ -106,24 +109,39 @@
     load_s.start()
     load_t = pltpu.make_async_copy(taps_hbm.at[j], taps, load_sem.at[2])
     load_t.start()
+    small = [(fcell_hbm, fcell), (fown_hbm, fown), (fpan_hbm, fpan), (farea_hbm, farea), (kx_hbm, kx), (kx10_hbm, kx10), (sx_hbm, sx)]
+    small = [pltpu.make_async_copy(a, b, load_sem.at[3 + i]) for i, (a, b) in enumerate(small)]
+    for load in small:
+        load.start()
 
     barrier = pltpu.get_barrier_semaphore()
-    for k in range(1, GROUP):
-        pl.semaphore_signal(barrier, inc=1, device_id=(d, (s + k) % GROUP), device_id_type=MESH)
-
-    @pl.when(d != 0)
-    def _():
-        pl.semaphore_signal(barrier, inc=1, device_id=(0, s), device_id_type=MESH)
-        pl.semaphore_wait(barrier, GROUP - 1)
 
     @pl.when(d == 0)
     def _():
-        pl.semaphore_wait(barrier, GROUP - 1 + DIRS - 1)
-
-    @pl.when(d == 0)
-    def _():
+        for k in range(GROUP):
+            pl.semaphore_signal(barrier, inc=1, device_id=(1, (s + k) % GROUP), device_id_type=MESH)
+        pl.semaphore_wait(barrier, DIRS - 1)
         for k in range(1, DIRS):
             remote(prec.at[0], pb, s_p.at[k], r_p, (k, s)).start()
+        own = pltpu.make_async_copy(prec.at[0], pb, l_p)
+        own.start()
+        own.wait()
+        pl.semaphore_wait(go, 1)
+
+    @pl.when(d != 0)
+    def _():
+        pl.semaphore_signal(barrier, inc=1, device_id=(0, s), device_id_type=MESH)
+        for k in range(1, GROUP):
+            pl.semaphore_signal(barrier, inc=1, device_id=(d, (s + k) % GROUP), device_id_type=MESH)
+
+    @pl.when(d == 1)
+    def _():
+        pl.semaphore_wait(barrier, 2 * GROUP - 1)
+        pl.semaphore_signal(go, inc=1, device_id=(0, s), device_id_type=MESH)
+
+    @pl.when(d > 1)
+    def _():
+        pl.semaphore_wait(barrier, GROUP - 1)
 
     for t in range(TILES):
         @pl.when(s != owners[t])
@@ -144,6 +162,8 @@
     def column(row):
         return jnp.transpose(jnp.broadcast_to(row, (128, FACADES)))
 
+    for load in small:
+        load.wait()
     cell = column(fcell[...])
     lane = lax.broadcasted_iota(jnp.int32, (FACADES, 128), 1)
     selrow[...] = jnp.where((cell >> 9) == lane, 1.0, 0.0)
@@ -154,12 +174,6 @@
         lax.broadcasted_iota(jnp.int32, (GROUP, FACADES), 0) == jnp.broadcast_to(fown[...], (GROUP, FACADES)), 1.0, 0.0
     )
 
-    @pl.when(d == 0)
-    def _():
-        own = pltpu.make_async_copy(prec.at[0], pb, l_p)
-        own.start()
-        own.wait()
-
     @pl.when(d != 0)
     def _():
         remote(prec.at[0], pb, s_p.at[0], r_p, (0, s)).wait_recv()
@@ -174,47 +188,13 @@
         @pl.when(s == owners[t])
         def _(t=t, c=c, k=k):
             col[pl.ds(pl.multiple_of(8 * s, 8), 8), :] = pb[c, :, 128 * k : 128 * (k + 1)]
-            rr[pl.ds(pl.multiple_of(8 * s, 8), 8), :] = rot[0, :, 0:128]
-
-    @pl.when(is_owner)
-    def _():
-        part = pl.ds(0, 8 * (GROUP - 1))
-        remote(rr.at[part], rr.at[part], s_r, r_r, (d, (s + 1) % GROUP)).wait_recv()
-        q = rr[...] >> 9
-        lane = lax.broadcasted_iota(jnp.int32, (NY, 128), 1)
-        low = jnp.where(q == lane, 1.0, 0.0)
-        high = jnp.where(q - 128 == lane, 1.0, 0.0)
-        pbuf[0:8, :] = jnp.zeros((8, 128), jnp.float32)
-        pbuf[NY : NY + 8, :] = jnp.zeros((8, 128), jnp.float32)
-        remote(col.at[part], col.at[part], s_t, r_t, (d, (s + 1) % GROUP)).wait_recv()
-        pbuf[4 : NY + 4, :] = dot(low, col[0:128, :]) + dot(high, col[128:256, :])
-
-        def send(k, carry):
-            to = (s + k) % GROUP
-            remote(pbuf.at[pl.ds(8 * to, 16)], infl.at[my_tile], s_i, r_i, (d, to)).start()
-            return carry
-
-        lax.fori_loop(1, GROUP, send, 0)
-        infl[my_tile] = pbuf[pl.ds(pl.multiple_of(8 * s, 8), 16), :]
+            tile = pltpu.make_async_copy(rot.at[0, :, pl.ds(0, 128)], rr.at[pl.ds(8 * s, 8)], l_p)
+            tile.start()
+            tile.wait()
 
     load_u.wait()
     for edge in edges:
         edge.wait()
-
-    @pl.when(is_owner)
-    def _():
-        part = pl.ds(0, TILES - 1)
-        remote(infl.at[part], infl.at[part], s_i, r_i, (d, (s + 1) % GROUP)).wait_recv()
-
-    @pl.when(jnp.logical_not(is_owner))
-    def _():
-        remote(infl, infl, s_i, r_i, (d, (s + 1) % GROUP)).wait_recv()
-
-    for t in range(TILES):
-        c, k = t // 4, t % 4
-        for r in range(ROWS + 4):
-            uext[c, r, 0:1, 128 * k : 128 * (k + 1)] = infl[t, r + 2 : r + 3, :]
-
     blank = jnp.zeros((2, NX, NZ), jnp.float32)
 
     @pl.when(s == 0)
@@ -239,7 +219,8 @@
             + uext[1, r] * (yplus - yminus) * 2.0
             + uext[2, r] * (zplus - zminus) * 0.5
         )
-        ust[c, r - 1] = q + time_step * (viscosity * lap - advect)
+        result = q + time_step * (viscosity * lap - advect)
+        ust[c, r - 1] = jnp.where(lax.broadcasted_iota(jnp.int32, (NX, NZ), 0) < 2, 0.0, result)
 
     def row_y(r, carry):
         tentative(1, r)
@@ -277,66 +258,159 @@
     for k in range(4):
         xh[k] = modes[:, 128 * k : 128 * (k + 1)].reshape(ROWS, NX, QUARTER)
 
-    for dk in range(1, 4):
-        k = (j + dk) % 4
-        remote(xh.at[k], win.at[pl.ds(HALO + 8 * j, 8)], s_x, r_x, (d, 4 * zc + k)).start()
     above = 4 * ((zc + 1) % LEVELS)
     below = 4 * ((zc + LEVELS - 1) % LEVELS)
 
-    @pl.when(j >= 2)
-    def _():
-        for k in range(4):
-            remote(xh.at[k], win.at[pl.ds(8 * j - 12, 8)], s_x, r_x, (d, above + k)).start()
-
-    @pl.when(j == 1)
-    def _():
-        for k in range(4):
-            remote(xh.at[k, pl.ds(4, 4)], win.at[pl.ds(0, 4)], s_x, r_x, (d, above + k)).start()
-
-    @pl.when(j <= 1)
-    def _():
-        for k in range(4):
-            remote(xh.at[k], win.at[pl.ds(HALO + 32 + 8 * j, 8)], s_x, r_x, (d, below + k)).start()
-
-    @pl.when(j == 2)
-    def _():
-        for k in range(4):
-            remote(xh.at[k, pl.ds(0, 4)], win.at[pl.ds(WINDOW - 4, 4)], s_x, r_x, (d, below + k)).start()
+    def to_level(src, dst, send, recv):
+        for dk in range(1, 4):
+            k = (j + dk) % 4
+            remote(src.at[k], dst(3 + j), send, recv, (d, 4 * zc + k)).start()
+
+        @pl.when(j >= 1)
+        def _():
+            for k in range(4):
+                remote(src.at[k], dst(j - 1), send, recv, (d, above + k)).start()
+
+        @pl.when(j <= 2)
+        def _():
+            for k in range(4):
+                remote(src.at[k], dst(7 + j), send, recv, (d, below + k)).start()
+
+    to_level(xh, lambda b: win.at[pl.ds(8 * b, 8)], s_x, r_x)
+
+    for c in range(3):
+        for x in (1, 2):
+            for r in range(ROWS + 4):
+                near_x[c, x - 1, r + 2 : r + 3, :] = uext[c, r, x : x + 1, :]
+
+    @pl.when(is_owner)
+    def _():
+        part = pl.ds(0, 8 * (GROUP - 1))
+        remote(rr.at[part], rr.at[part], s_r, r_r, (d, (s + 1) % GROUP)).wait_recv()
+        q = rr[...] >> 9
+        lane = lax.broadcasted_iota(jnp.int32, (NY, 128), 1)
+        low = jnp.where(q == lane, 1.0, 0.0)
+        high = jnp.where(q - 128 == lane, 1.0, 0.0)
+        pbuf[0:8, :] = jnp.zeros((8, 128), jnp.float32)
+        pbuf[NY : NY + 8, :] = jnp.zeros((8, 128), jnp.float32)
+        remote(col.at[part], col.at[part], s_t, r_t, (d, (s + 1) % GROUP)).wait_recv()
+        pbuf[4 : NY + 4, :] = dot(low, col[0:128, :]) + dot(high, col[128:256, :])
+
+        def send(k, carry):
+            to = (s + k) % GROUP
+            remote(pbuf.at[pl.ds(8 * to, 16)], infl.at[my_tile], s_i, r_i, (d, to)).start()
+            return carry
+
+        lax.fori_loop(1, GROUP, send, 0)
+        infl[my_tile] = pbuf[pl.ds(pl.multiple_of(8 * s, 8), 16), :]
+
+    @pl.when(is_owner)
+    def _():
+        part = pl.ds(0, TILES - 1)
+        remote(infl.at[part], infl.at[part], s_i, r_i, (d, (s + 1) % GROUP)).wait_recv()
+
+    @pl.when(jnp.logical_not(is_owner))
+    def _():
+        remote(infl, infl, s_i, r_i, (d, (s + 1) % GROUP)).wait_recv()
+
+    height = (2 * ROWS, NZ)
+    row = lax.broadcasted_iota(jnp.int32, height, 0)
+    outside = ((s == 0) & (row == 3)) | ((s == GROUP - 1) & (row == ROWS + 4))
+
+    def y_next(q):
+        return pltpu.roll(q, 2 * ROWS - 1, 0)
+
+    def y_last(q):
+        return pltpu.roll(q, 1, 0)
+
+    at0 = [jnp.concatenate([infl[4 * c + k] for k in range(4)], axis=1) for c in range(3)]
+    at1 = [near_x[c, 0] for c in range(3)]
+    for x, (field, ahead, behind) in enumerate(((at0, at1, at0), (at1, [near_x[c, 1] for c in range(3)], at0))):
+        for c in range(3):
+            q, xplus, xminus = field[c], ahead[c], behind[c]
+            yplus, yminus = y_next(q), y_last(q)
+            zplus, zminus = shift_lanes(q, 1), shift_lanes(q, -1)
+            lap = xplus + xminus + zplus + zminus + 16.0 * (yplus + yminus) - 36.0 * q
+            advect = (
+                field[0] * (xplus - xminus) * 0.5
+                + field[1] * (yplus - yminus) * 2.0
+                + field[2] * (zplus - zminus) * 0.5
+            )
+            result = q + time_step * (viscosity * lap - advect)
+            inlet[x, c] = jnp.where(outside, 0.0, result) if c == 1 else result
+
+    def beside(x):
+        qy, qz = inlet[x, 1], inlet[x, 2]
+        return (y_next(qy) - y_last(qy)) * 2.0 + (shift_lanes(qz, 1) - shift_lanes(qz, -1)) * 0.5
+
+    v0, v1 = inlet[0, 0], inlet[1, 0]
+    parts = [(v1 - v0) * 0.5 + beside(0), beside(1) - v0 * 0.5, v1 * -0.5]
+    late = dot(jnp.concatenate([part[4:12] for part in parts], axis=0), sz[...])
+    for k in range(4):
+        xl[k] = late[:, 128 * k : 128 * (k + 1)]
+    to_level(xl, lambda b: wl.at[b], s_l, r_l)
+
+    for x in range(2):
+        for c in range(3):
+            for r in range(ROWS):
+                ust[c, r + 1, x : x + 1, :] = inlet[x, c, r + 4 : r + 5, :]
 
     win[pl.ds(HALO + 8 * j, 8)] = xh[j]
+    wl[3 + j] = xl[j]
     load_t.wait()
     others = pl.ds(0, WINDOW - 8)
     remote(win.at[others], win.at[others], s_x, r_x, (d, (s + 1) % GROUP)).wait_recv()
+    nine = pl.ds(0, 9)
+    remote(wl.at[nine], wl.at[nine], s_l, r_l, (d, (s + 1) % GROUP)).wait_recv()
+
+    def join(b, carry):
+        block = wl[b]
+        for r in range(ROWS):
+            total = win[8 * b + r]
+            for x in range(LATE):
+                total = total + jnp.broadcast_to(block[8 * x + r : 8 * x + r + 1, :], (NX, QUARTER)) * sx[x]
+            win[8 * b + r] = total
+        return carry
+
+    lax.fori_loop(0, WINDOW // 8, join, 0)
 
     @pl.when(zc == 0)
     def _():
         win[HALO - 1] = jnp.zeros((NX, QUARTER), jnp.float32)
-        for i in range(1, HALO):
+        for i in range(1, ITERS):
             win[HALO - 1 - i] = -win[HALO - 1 + i]
 
     @pl.when(zc == LEVELS - 1)
     def _():
         win[HALO + 32] = jnp.zeros((NX, QUARTER), jnp.float32)
-        for i in range(1, HALO):
+        for i in range(1, ITERS):
             win[HALO + 32 + i] = -win[HALO + 32 - i]
 
-    def filter_row(y, carry):
-        total = taps[0] * win[y + 19]
-        for i in range(1, ITERS):
-            total = total + taps[i] * (win[y + 19 + i] + win[y + 19 - i])
-        ph[y] = total
-        return carry
-
-    lax.fori_loop(0, 34, filter_row, 0)
-
-    for dk in range(1, 4):
-        k = (j + dk) % 4
-        remote(ph.at[pl.ds(8 * k, 10)], bk.at[j], s_b, r_b, (d, 4 * zc + k)).start()
-    bk[j] = ph[pl.ds(8 * j, 10)]
-    back = pl.ds(0, 3)
-    remote(bk.at[back], bk.at[back], s_b, r_b, (d, (s + 1) % GROUP)).wait_recv()
-
-    spread = sum(dot(bk[k].reshape(10 * NX, QUARTER), sz[128 * k : 128 * (k + 1), :]) for k in range(4))
+    backs = []
+    for dk in (1, 2, 3, 0):
+        first = 8 * ((j + dk) % 4)
+
+        def filter_row(y, carry, first=first, dk=dk):
+            at = first + y + HALO - 1
+            total = taps[0] * win[at]
+            for i in range(1, ITERS):
+                total = total + taps[i] * (win[at + i] + win[at - i])
+            ph[dk, y] = total
+            return carry
+
+        lax.fori_loop(0, ROWS + 2, filter_row, 0)
+        if dk:
+            back = remote(ph.at[dk], bk.at[dk], s_b.at[dk], r_b.at[dk], (d, 4 * zc + (j + dk) % 4))
+            back.start()
+            backs.append(back)
+
+    def quarter(block, k):
+        return dot(block.reshape(10 * NX, QUARTER), sz[pl.ds(pl.multiple_of(128 * k, 128), 128), :])
+
+    spread = quarter(ph[0], j)
+    for dk in (1, 2, 3):
+        backs[dk - 1].wait_recv()
+        spread = spread + quarter(bk[dk], (j + 4 - dk) % 4)
     phi[...] = dot(kx10[...], spread).reshape(10, NX, NZ)
 
     @pl.when(s == 0)
@@ -396,15 +470,28 @@
     @pl.when((j == 0) | (j == 3))
     def _():
         remote(win.at[pl.ds(0, 56)], win.at[pl.ds(0, 56)], s_x, r_x, up).wait_send()
+        remote(wl.at[pl.ds(0, 7)], wl.at[pl.ds(0, 7)], s_l, r_l, up).wait_send()
 
     @pl.when((j == 1) | (j == 2))
     def _():
         remote(win, win, s_x, r_x, up).wait_send()
-
-    remote(bk.at[back], bk.at[back], s_b, r_b, up).wait_send()
+        remote(win.at[pl.ds(0, 8)], win.at[pl.ds(0, 8)], s_x, r_x, up).wait_send()
+        remote(wl, wl, s_l, r_l, up).wait_send()
+        remote(wl.at[0], wl.at[0], s_l, r_l, up).wait_send()
+
+    for back in backs:
+        back.wait_send()
     rest = pl.ds(0, GROUP - 1)
     remote(frecv.at[rest], frecv.at[rest], s_f, r_f, up).wait()
     fout[...] = jnp.sum(frecv[...], axis=0)
+
+
+def write_out(a, b, c, a_hbm, b_hbm, c_hbm, sem):
+    copies = [pltpu.make_async_copy(x, y, sem.at[i]) for i, (x, y) in enumerate(((a, a_hbm), (b, b_hbm), (c, c_hbm)))]
+    for copy in copies:
+        copy.start()
+    for copy in copies:
+        copy.wait()
 
 
 def body(velocity, precursor, rot_map, facade_cell, facade_owner, facade_panel, facade_area):
@@ -415,20 +502,32 @@
         jnp.asarray(sweep_taps(), f32),
         jnp.asarray(np.kron(np.eye(ROWS), across), f32),
         jnp.asarray(np.kron(np.eye(ROWS + 2), across), f32),
+        jnp.asarray(np.broadcast_to(across[:LATE, :, None], (LATE, NX, QUARTER)), f32),
     ]
-    far = pl.BlockSpec(memory_space=pl.ANY)
+    far = pl.BlockSpec(memory_space=pltpu.HBM)
     near = pl.BlockSpec(memory_space=pltpu.VMEM)
     dma = pltpu.SemaphoreType.DMA
-    return pl.pallas_call(
+    result = pl.pallas_call(
         kernel,
         out_shape=(
             jax.ShapeDtypeStruct((1, 3, ROWS, NX, NZ), f32),
             jax.ShapeDtypeStruct((1, ROWS, NX, NZ), f32),
             jax.ShapeDtypeStruct((1, PAN_DEV), f32),
         ),
-        in_specs=[far, far, near, near, near, near, near, far, far, near, near],
+        in_specs=[far] * 12,
         out_specs=(near, near, near),
         scratch_shapes=[
+            pltpu.VMEM((1, FACADES), jnp.int32),
+            pltpu.VMEM((1, FACADES), jnp.int32),
+            pltpu.VMEM((1, FACADES), jnp.int32),
+            pltpu.VMEM((1, FACADES), f32),
+            pltpu.VMEM((ROWS * NX, ROWS * NX), f32),
+            pltpu.VMEM(((ROWS + 2) * NX, (ROWS + 2) * NX), f32),
+            pltpu.VMEM((LATE, NX, QUARTER), f32),
+            pltpu.VMEM((3, 2, 2 * ROWS, NZ), f32),
+            pltpu.VMEM((2, 3, 2 * ROWS, NZ), f32),
+            pltpu.VMEM((4, LATE * ROWS, QUARTER), f32),
+            pltpu.VMEM((WINDOW // 8, LATE * ROWS, QUARTER), f32),
             pltpu.VMEM((3, ROWS + 4, NX, NZ), f32),
             pltpu.VMEM((3, ROWS, NZ), f32),
             pltpu.VMEM((NY, 128), jnp.int32),
@@ -440,7 +539,7 @@
             pltpu.VMEM((ITERS, NX, QUARTER), f32),
             pltpu.VMEM((4, ROWS, NX, QUARTER), f32),
             pltpu.VMEM((WINDOW, NX, QUARTER), f32),
-            pltpu.VMEM((34, NX, QUARTER), f32),
+            pltpu.VMEM((4, ROWS + 2, NX, QUARTER), f32),
             pltpu.VMEM((4, ROWS + 2, NX, QUARTER), f32),
             pltpu.VMEM((ROWS + 2, NX, NZ), f32),
             pltpu.VMEM((GROUP, 1, PAN_DEV), f32),
@@ -450,15 +549,22 @@
             pltpu.VMEM((FACADES, 128), jnp.int32),
             pltpu.VMEM((FACADES, 128), f32),
             pltpu.VMEM((GROUP, FACADES), f32),
-            dma((3,)), dma((4,)), dma((4,)), dma((DIRS,)),
-            dma, dma, dma, dma, dma, dma, dma, dma, dma, dma, dma, dma, dma, dma,
+            dma((10,)), pltpu.SemaphoreType.REGULAR, dma((4,)), dma((4,)), dma((DIRS,)),
+            dma, dma, dma, dma, dma, dma, dma, dma, dma, dma, dma, dma((4,)), dma((4,)), dma, dma, dma,
         ],
         compiler_params=pltpu.CompilerParams(
-            collective_id=0, has_side_effects=True, vmem_limit_bytes=48 << 20
+            collective_id=0, has_side_effects=True, vmem_limit_bytes=60 << 20
         ),
     )(
         velocity, precursor, rot_map, facade_cell, facade_owner.reshape(1, FACADES), facade_panel, facade_area, *constants
     )
+    return pl.pallas_call(
+        write_out,
+        out_shape=[jax.ShapeDtypeStruct(x.shape, x.dtype) for x in result],
+        in_specs=[near] * 3,
+        out_specs=[far] * 3,
+        scratch_shapes=[dma((3,))],
+    )(*result)
 
 
 def solution(mesh):

time: 78.8 us -> 64.9 us (0.82)
  the two profiles are of different devices: /device:TPU:33 before, /device:TPU:1 now
where the time goes in v2:
time: 64.9 us; the launch traced here: 64.6 us
  Pallas kernels  64 us (99%)
    pallas_call x1, Pallas kernels, body(): pl.pallas_call(kernel, out_shape=(jax.ShapeDtypeStruct((1, 3, ROWS, NX, N...  61.8 us
    pallas_call x1, Pallas kernels, body(): pl.pallas_call(write_out, out_shape=[jax.ShapeDtypeStruct(x.shape, x.dtyp...  2.21 us

profile of v2, /device:TPU:1, one launch (start us, length us, event | category | flops | bytes accessed | tf_op | source)
XLA Modules:
  0.0 64.6 jit_solution(17611109612544084481)
XLA Ops:
  0.6 61.8 %shard_map.139 = (f32[1,3,8,16,512]{4,3,2,1,0:T(8,128)}, f32[1,8,16,512]{3,2,1,0:T(8,128)}, f32[1,128]{1,0:T(1,128)}) custom-call(f32[1,3,8,16,512]{4,3,2,1,0:T(8,128)} %vel.1, f32[1,3,8,512]{3,2,1,0:T(8,128)} %prec.1, s32[1,8,512]{2,1,0:T(8,128)} %rot.1, s32[1,256]{1,0:T(1,128)} %fcell_hbm.1, s32[1,256]{1,0:T(1,128)} %bitcast.1, s32[1,256]{1,0:T(1,128)} %fpan_hbm.1, ...), custom_call_target="tpu_custom_call" | custom-call | tf_op jit(solution)/shard_map/pallas_call | solution.py:510
  62.4 2.2 %shard_map.140 = (f32[1,3,8,16,512]{4,3,2,1,0:T(8,128)}, f32[1,8,16,512]{3,2,1,0:T(8,128)}, f32[1,128]{1,0:T(1,128)}) custom-call(f32[1,3,8,16,512]{4,3,2,1,0:T(8,128)} %get-tuple-element.6.a, f32[1,8,16,512]{3,2,1,0:T(8,128)} %get-tuple-element.7.b, f32[1,128]{1,0:T(1,128)} %get-tuple-element.8.c), custom_call_target="tpu_custom_call" | custom-call | tf_op jit(solution)/shard_map/pallas_call | solution.py:561

commit v3 on v2

--- a/solution.py
+++ b/solution.py
@@ -85,14 +85,35 @@
     return lax.dot_general(a, b, (((1,), (0,)), ((), ())), precision=EXACT, preferred_element_type=jnp.float32)
 
 
+def bdot(a, b):
+    return lax.dot_general(a, b, (((1,), (0,)), ((), ())), preferred_element_type=jnp.float32)
+
+
+def thirds(x):
+    high = x.astype(jnp.bfloat16)
+    rest = x - high.astype(jnp.float32)
+    middle = rest.astype(jnp.bfloat16)
+    return high, middle, (rest - middle.astype(jnp.float32)).astype(jnp.bfloat16)
+
+
+def dot_thirds(x, parts):
+    n = x.shape[0]
+    high, middle, low = thirds(x)
+    a = bdot(jnp.concatenate([high, middle, low], axis=0), parts(0))
+    b = bdot(jnp.concatenate([high, middle], axis=0), parts(1))
+    c = bdot(high, parts(2))
+    return a[:n] + ((a[n : 2 * n] + b[:n]) + (a[2 * n :] + (b[n:] + c)))
+
+
 def kernel(
     vel, prec, rot, fcell_hbm, fown_hbm, fpan_hbm, farea_hbm, sz_hbm, taps_hbm, kx_hbm, kx10_hbm, sx_hbm,
-    vout, pout, fout,
+    vel_hbm, pot_hbm, fout,
+    vout,
     fcell, fown, fpan, farea, kx, kx10, sx,
     near_x, inlet, xl, wl,
     uext, pb, rr, col, pbuf, infl, ust, sz, taps, xh, win, ph, bk, phi, fterm, frecv,
-    selrow, colz, colp, cola, ohown,
-    load_sem, go, s_u, r_u, s_p, r_p, s_r, r_r, s_t, r_t, s_i, r_i, s_x, r_x, s_l, r_l, s_b, r_b, s_f, r_f, l_p,
+    fa, fz, onpan, ohown,
+    load_sem, go, s_u, r_u, s_p, r_p, s_r, r_r, s_t, r_t, s_i, r_i, s_x, r_x, s_l, r_l, s_b, r_b, s_f, r_f, s_c, r_c, l_p, out_sem,
 ):
     d = lax.axis_index("dir")
     s = lax.axis_index("space")
@@ -109,7 +130,8 @@
     load_s.start()
     load_t = pltpu.make_async_copy(taps_hbm.at[j], taps, load_sem.at[2])
     load_t.start()
-    small = [(fcell_hbm, fcell), (fown_hbm, fown), (fpan_hbm, fpan), (farea_hbm, farea), (kx_hbm, kx), (kx10_hbm, kx10), (sx_hbm, sx)]
+    lists = [(fcell_hbm, fcell), (fown_hbm, fown), (fpan_hbm, fpan), (farea_hbm, farea)]
+    small = [(a, b.at[j]) for a, b in lists] + [(kx_hbm, kx), (kx10_hbm, kx10), (sx_hbm, sx)]
     small = [pltpu.make_async_copy(a, b, load_sem.at[3 + i]) for i, (a, b) in enumerate(small)]
     for load in small:
         load.start()
@@ -159,20 +181,9 @@
     for edge in edges:
         edge.start()
 
-    def column(row):
-        return jnp.transpose(jnp.broadcast_to(row, (128, FACADES)))
-
-    for load in small:
-        load.wait()
-    cell = column(fcell[...])
-    lane = lax.broadcasted_iota(jnp.int32, (FACADES, 128), 1)
-    selrow[...] = jnp.where((cell >> 9) == lane, 1.0, 0.0)
-    colz[...] = cell & 511
-    colp[...] = column(fpan[...])
-    cola[...] = column(farea[...])
-    ohown[...] = jnp.where(
-        lax.broadcasted_iota(jnp.int32, (GROUP, FACADES), 0) == jnp.broadcast_to(fown[...], (GROUP, FACADES)), 1.0, 0.0
-    )
+    for dk in range(1, 4):
+        for a, b in lists:
+            remote(a, b.at[j], s_c, r_c, (d, 4 * zc + (j + dk) % 4)).start()
 
     @pl.when(d != 0)
     def _():
@@ -192,7 +203,31 @@
             tile.start()
             tile.wait()
 
+    @pl.when(is_owner)
+    def _():
+        part = pl.ds(0, 8 * (GROUP - 1))
+        remote(rr.at[part], rr.at[part], s_r, r_r, (d, (s + 1) % GROUP)).wait_recv()
+        q = rr[...] >> 9
+        lane = lax.broadcasted_iota(jnp.int32, (NY, 128), 1)
+        chosen = jnp.concatenate([jnp.where(q == lane, 1.0, 0.0), jnp.where(q - 128 == lane, 1.0, 0.0)], axis=1)
+        chosen = chosen.astype(jnp.bfloat16)
+        pbuf[0:8, :] = jnp.zeros((8, 128), jnp.float32)
+        pbuf[NY : NY + 8, :] = jnp.zeros((8, 128), jnp.float32)
+        remote(col.at[part], col.at[part], s_t, r_t, (d, (s + 1) % GROUP)).wait_recv()
+        rows = bdot(chosen, jnp.concatenate(thirds(col[...]), axis=1))
+        pbuf[4 : NY + 4, :] = rows[:, 0:128] + (rows[:, 128:256] + rows[:, 256:384])
+
+        def send(i, carry):
+            to = (s + 16 + ((i + 1) // 2) * (2 * (i % 2) - 1)) % GROUP
+            remote(pbuf.at[pl.ds(8 * to, 16)], infl.at[my_tile], s_i, r_i, (d, to)).start()
+            return carry
+
+        lax.fori_loop(0, GROUP - 1, send, 0)
+        infl[my_tile] = pbuf[pl.ds(pl.multiple_of(8 * s, 8), 16), :]
+
     load_u.wait()
+    for load in small:
+        load.wait()
     for edge in edges:
         edge.wait()
     blank = jnp.zeros((2, NX, NZ), jnp.float32)
@@ -254,7 +289,7 @@
     lax.fori_loop(0, ROWS, row_div, 0)
 
     load_s.wait()
-    modes = dot(dot(kx[...], phi[0:ROWS].reshape(ROWS * NX, NZ)), sz[...])
+    modes = dot_thirds(dot(kx[...], phi[0:ROWS].reshape(ROWS * NX, NZ)), lambda i: sz[i])
     for k in range(4):
         xh[k] = modes[:, 128 * k : 128 * (k + 1)].reshape(ROWS, NX, QUARTER)
 
@@ -282,27 +317,6 @@
         for x in (1, 2):
             for r in range(ROWS + 4):
                 near_x[c, x - 1, r + 2 : r + 3, :] = uext[c, r, x : x + 1, :]
-
-    @pl.when(is_owner)
-    def _():
-        part = pl.ds(0, 8 * (GROUP - 1))
-        remote(rr.at[part], rr.at[part], s_r, r_r, (d, (s + 1) % GROUP)).wait_recv()
-        q = rr[...] >> 9
-        lane = lax.broadcasted_iota(jnp.int32, (NY, 128), 1)
-        low = jnp.where(q == lane, 1.0, 0.0)
-        high = jnp.where(q - 128 == lane, 1.0, 0.0)
-        pbuf[0:8, :] = jnp.zeros((8, 128), jnp.float32)
-        pbuf[NY : NY + 8, :] = jnp.zeros((8, 128), jnp.float32)
-        remote(col.at[part], col.at[part], s_t, r_t, (d, (s + 1) % GROUP)).wait_recv()
-        pbuf[4 : NY + 4, :] = dot(low, col[0:128, :]) + dot(high, col[128:256, :])
-
-        def send(k, carry):
-            to = (s + k) % GROUP
-            remote(pbuf.at[pl.ds(8 * to, 16)], infl.at[my_tile], s_i, r_i, (d, to)).start()
-            return carry
-
-        lax.fori_loop(1, GROUP, send, 0)
-        infl[my_tile] = pbuf[pl.ds(pl.multiple_of(8 * s, 8), 16), :]
 
     @pl.when(is_owner)
     def _():
@@ -345,15 +359,34 @@
 
     v0, v1 = inlet[0, 0], inlet[1, 0]
     parts = [(v1 - v0) * 0.5 + beside(0), beside(1) - v0 * 0.5, v1 * -0.5]
-    late = dot(jnp.concatenate([part[4:12] for part in parts], axis=0), sz[...])
+    rows = [part[4:12] for part in parts] + [jnp.zeros((ROWS, NZ), jnp.float32)]
+    late = dot_thirds(jnp.concatenate(rows, axis=0), lambda i: sz[i])
     for k in range(4):
-        xl[k] = late[:, 128 * k : 128 * (k + 1)]
+        xl[k] = late[0 : LATE * ROWS, 128 * k : 128 * (k + 1)]
     to_level(xl, lambda b: wl.at[b], s_l, r_l)
 
     for x in range(2):
         for c in range(3):
             for r in range(ROWS):
                 ust[c, r + 1, x : x + 1, :] = inlet[x, c, r + 4 : r + 5, :]
+
+    remote(xl.at[0], xl.at[0], s_c, r_c, up).wait_recv()
+    wide = lax.broadcasted_iota(jnp.int32, (FACADES, 128), 1)
+    tall = lax.broadcasted_iota(jnp.int32, (FACADES, NZ), 1)
+    mine = pl.ds(pl.multiple_of(128 * j, 128), 128)
+
+    def prepare(q, carry):
+        cell = jnp.transpose(jnp.broadcast_to(fcell[q], (8, FACADES)))[:, 0:1]
+        panel = jnp.transpose(jnp.broadcast_to(fpan[q], (8, FACADES)))[:, 0:1]
+        area = jnp.transpose(jnp.broadcast_to(farea[q], (8, FACADES)))[:, 0:1]
+        fa[q] = dot(jnp.where((cell >> 9) == wide, 1.0, 0.0), kx[...])
+        at = jnp.where((cell & 511) == tall, 1.0, 0.0).astype(jnp.bfloat16)
+        fz[q] = (bdot(at, sz[0, :, mine]) + (bdot(at, sz[1, :, mine]) + bdot(at, sz[2, :, mine]))) * area
+        onpan[q] = jnp.where(panel == wide, 1.0, 0.0)
+        ohown[q] = jnp.where(lax.broadcasted_iota(jnp.int32, (GROUP, FACADES), 0) == fown[q], 1.0, 0.0)
+        return carry
+
+    lax.fori_loop(0, 4, prepare, 0)
 
     win[pl.ds(HALO + 8 * j, 8)] = xh[j]
     wl[3 + j] = xl[j]
@@ -387,8 +420,8 @@
             win[HALO + 32 + i] = -win[HALO + 32 - i]
 
     backs = []
-    for dk in (1, 2, 3, 0):
-        first = 8 * ((j + dk) % 4)
+    for dk in (2, 3, 1, 0):
+        first = 8 * (j ^ dk)
 
         def filter_row(y, carry, first=first, dk=dk):
             at = first + y + HALO - 1
@@ -400,17 +433,36 @@
 
         lax.fori_loop(0, ROWS + 2, filter_row, 0)
         if dk:
-            back = remote(ph.at[dk], bk.at[dk], s_b.at[dk], r_b.at[dk], (d, 4 * zc + (j + dk) % 4))
+            back = remote(ph.at[dk], bk.at[dk], s_b.at[dk], r_b.at[dk], (d, 4 * zc + (j ^ dk)))
             back.start()
             backs.append(back)
 
+    terms = jnp.zeros((GROUP, PAN_DEV), jnp.float32)
+    for dk in range(4):
+        q = j ^ dk
+        lines = dot(fa[q], ph[dk, 1 : ROWS + 1].reshape(ROWS * NX, QUARTER))
+        value = jnp.sum(lines * fz[q], axis=1, keepdims=True)
+        terms = terms + dot(ohown[q], onpan[q] * value)
+    for o in range(GROUP):
+        fterm[o] = terms[o : o + 1, :]
+
+    def send_terms(i, carry):
+        to = (s + 16 + ((i + 1) // 2) * (2 * (i % 2) - 1)) % GROUP
+        remote(fterm.at[to], frecv.at[s], s_f, r_f, (d, to)).start()
+        return carry
+
+    lax.fori_loop(0, GROUP - 1, send_terms, 0)
+    frecv[s] = fterm[s]
+
     def quarter(block, k):
-        return dot(block.reshape(10 * NX, QUARTER), sz[pl.ds(pl.multiple_of(128 * k, 128), 128), :])
+        rows = pl.ds(pl.multiple_of(128 * k, 128), 128)
+        return dot_thirds(block.reshape(10 * NX, QUARTER), lambda i: sz[i, rows, :])
 
     spread = quarter(ph[0], j)
     for dk in (1, 2, 3):
-        backs[dk - 1].wait_recv()
-        spread = spread + quarter(bk[dk], (j + 4 - dk) % 4)
+        arrived = backs[(2, 3, 1).index(dk)]
+        arrived.wait_recv()
+        spread = spread + quarter(bk[dk], j ^ dk)
     phi[...] = dot(kx10[...], spread).reshape(10, NX, NZ)
 
     @pl.when(s == 0)
@@ -420,32 +472,21 @@
     @pl.when(s == GROUP - 1)
     def _():
         phi[ROWS + 1] = jnp.zeros((NX, NZ), jnp.float32)
-
-    lines = dot(selrow[...], phi[1 : ROWS + 1].reshape(ROWS * NX, NZ))
-    zlane = lax.broadcasted_iota(jnp.int32, (FACADES, NZ), 1)
-    value = jnp.sum(jnp.where(colz[:, 0:1] == zlane, lines, 0.0), axis=1, keepdims=True) * cola[:, 0:1]
-    lane = lax.broadcasted_iota(jnp.int32, (FACADES, 128), 1)
-    terms = dot(ohown[...], jnp.where(colp[...] == lane, value, 0.0))
-    for o in range(GROUP):
-        fterm[o] = terms[o : o + 1, :]
-
-    def send_terms(k, carry):
-        to = (s + k) % GROUP
-        remote(fterm.at[to], frecv.at[s], s_f, r_f, (d, to)).start()
-        return carry
-
-    lax.fori_loop(1, GROUP, send_terms, 0)
-    frecv[s] = fterm[s]
 
     def row_out(r, carry):
         q = phi[r + 1]
-        vout[0, 0, r] = ust[0, r + 1] - (shift_x(q, 1, empty) - shift_x(q, -1, empty)) * 0.5
-        vout[0, 1, r] = ust[1, r + 1] - (phi[r + 2] - phi[r]) * 2.0
-        vout[0, 2, r] = ust[2, r + 1] - (shift_lanes(q, 1) - shift_lanes(q, -1)) * 0.5
-        pout[0, r] = q
+        vout[0, r] = ust[0, r + 1] - (shift_x(q, 1, empty) - shift_x(q, -1, empty)) * 0.5
+        vout[1, r] = ust[1, r + 1] - (phi[r + 2] - phi[r]) * 2.0
+        vout[2, r] = ust[2, r + 1] - (shift_lanes(q, 1) - shift_lanes(q, -1)) * 0.5
         return carry
 
     lax.fori_loop(0, ROWS, row_out, 0)
+    outs = [
+        pltpu.make_async_copy(phi.at[pl.ds(1, ROWS)], pot_hbm.at[0], out_sem.at[0]),
+        pltpu.make_async_copy(vout, vel_hbm.at[0], out_sem.at[1]),
+    ]
+    for out in outs:
+        out.start()
 
     @pl.when(d == 0)
     def _():
@@ -454,6 +495,7 @@
 
     eight = pl.ds(0, 8 * (TILES - 1))
 
+    remote(xl.at[0], xl.at[0], s_c, r_c, up).wait_send()
     remote(rr.at[eight], rr.at[eight], s_r, r_r, up).wait_send()
     remote(col.at[eight], col.at[eight], s_t, r_t, up).wait_send()
 
@@ -484,21 +526,35 @@
     rest = pl.ds(0, GROUP - 1)
     remote(frecv.at[rest], frecv.at[rest], s_f, r_f, up).wait()
     fout[...] = jnp.sum(frecv[...], axis=0)
-
-
-def write_out(a, b, c, a_hbm, b_hbm, c_hbm, sem):
-    copies = [pltpu.make_async_copy(x, y, sem.at[i]) for i, (x, y) in enumerate(((a, a_hbm), (b, b_hbm), (c, c_hbm)))]
-    for copy in copies:
-        copy.start()
-    for copy in copies:
-        copy.wait()
+    for out in outs:
+        out.wait()
+
+
+def write_out(vel, pot, force, vel_out, pot_out, force_out, vbuf, pbuf, fbuf, into, out):
+    half = ROWS // 2
+    parts = [
+        (vel.at[0, c, pl.ds(r, half)], vbuf.at[c, pl.ds(r, half)], vel_out.at[0, c, pl.ds(r, half)])
+        for c in range(3)
+        for r in (0, half)
+    ]
+    parts += [(pot.at[0, pl.ds(r, half)], pbuf.at[pl.ds(r, half)], pot_out.at[0, pl.ds(r, half)]) for r in (0, half)]
+    parts.append((force, fbuf, force_out))
+    loads = [pltpu.make_async_copy(a, b, into.at[i]) for i, (a, b, _) in enumerate(parts)]
+    stores = [pltpu.make_async_copy(b, c, out.at[i]) for i, (_, b, c) in enumerate(parts)]
+    for load in loads:
+        load.start()
+    for load, store in zip(loads, stores):
+        load.wait()
+        store.start()
+    for store in stores:
+        store.wait()
 
 
 def body(velocity, precursor, rot_map, facade_cell, facade_owner, facade_panel, facade_area):
     f32 = jnp.float32
     across = sine_matrix(NX)
     constants = [
-        jnp.asarray(sine_matrix(NZ), f32),
+        jnp.stack(thirds(jnp.asarray(sine_matrix(NZ), f32))),
         jnp.asarray(sweep_taps(), f32),
         jnp.asarray(np.kron(np.eye(ROWS), across), f32),
         jnp.asarray(np.kron(np.eye(ROWS + 2), across), f32),
@@ -515,12 +571,13 @@
             jax.ShapeDtypeStruct((1, PAN_DEV), f32),
         ),
         in_specs=[far] * 12,
-        out_specs=(near, near, near),
+        out_specs=(far, far, near),
         scratch_shapes=[
-            pltpu.VMEM((1, FACADES), jnp.int32),
-            pltpu.VMEM((1, FACADES), jnp.int32),
-            pltpu.VMEM((1, FACADES), jnp.int32),
-            pltpu.VMEM((1, FACADES), f32),
+            pltpu.VMEM((3, ROWS, NX, NZ), f32),
+            pltpu.VMEM((4, 1, FACADES), jnp.int32),
+            pltpu.VMEM((4, 1, FACADES), jnp.int32),
+            pltpu.VMEM((4, 1, FACADES), jnp.int32),
+            pltpu.VMEM((4, 1, FACADES), f32),
             pltpu.VMEM((ROWS * NX, ROWS * NX), f32),
             pltpu.VMEM(((ROWS + 2) * NX, (ROWS + 2) * NX), f32),
             pltpu.VMEM((LATE, NX, QUARTER), f32),
@@ -535,7 +592,7 @@
             pltpu.VMEM((NY + 8, 128), f32),
             pltpu.VMEM((TILES, 16, 128), f32),
             pltpu.VMEM((3, ROWS + 2, NX, NZ), f32),
-            pltpu.VMEM((NZ, NZ), f32),
+            pltpu.VMEM((3, NZ, NZ), jnp.bfloat16),
             pltpu.VMEM((ITERS, NX, QUARTER), f32),
             pltpu.VMEM((4, ROWS, NX, QUARTER), f32),
             pltpu.VMEM((WINDOW, NX, QUARTER), f32),
@@ -544,13 +601,12 @@
             pltpu.VMEM((ROWS + 2, NX, NZ), f32),
             pltpu.VMEM((GROUP, 1, PAN_DEV), f32),
             pltpu.VMEM((GROUP, 1, PAN_DEV), f32),
-            pltpu.VMEM((FACADES, 128), f32),
-            pltpu.VMEM((FACADES, 128), jnp.int32),
-            pltpu.VMEM((FACADES, 128), jnp.int32),
-            pltpu.VMEM((FACADES, 128), f32),
-            pltpu.VMEM((GROUP, FACADES), f32),
+            pltpu.VMEM((4, FACADES, 128), f32),
+            pltpu.VMEM((4, FACADES, 128), f32),
+            pltpu.VMEM((4, FACADES, 128), f32),
+            pltpu.VMEM((4, GROUP, FACADES), f32),
             dma((10,)), pltpu.SemaphoreType.REGULAR, dma((4,)), dma((4,)), dma((DIRS,)),
-            dma, dma, dma, dma, dma, dma, dma, dma, dma, dma, dma, dma((4,)), dma((4,)), dma, dma, dma,
+            dma, dma, dma, dma, dma, dma, dma, dma, dma, dma, dma, dma((4,)), dma((4,)), dma, dma, dma, dma, dma, dma((2,)),
         ],
         compiler_params=pltpu.CompilerParams(
             collective_id=0, has_side_effects=True, vmem_limit_bytes=60 << 20
@@ -561,9 +617,16 @@
     return pl.pallas_call(
         write_out,
         out_shape=[jax.ShapeDtypeStruct(x.shape, x.dtype) for x in result],
-        in_specs=[near] * 3,
+        in_specs=[far] * 3,
         out_specs=[far] * 3,
-        scratch_shapes=[dma((3,))],
+        scratch_shapes=[
+            pltpu.VMEM((3, ROWS, NX, NZ), f32),
+            pltpu.VMEM((ROWS, NX, NZ), f32),
+            pltpu.VMEM((1, PAN_DEV), f32),
+            dma((9,)),
+            dma((9,)),
+        ],
+        compiler_params=pltpu.CompilerParams(vmem_limit_bytes=60 << 20),
     )(*result)
 
 

time: 64.9 us -> 56 us (0.86)
  the two profiles are of different devices: /device:TPU:1 before, /device:TPU:33 now
where the time goes in v3:
time: 56 us; the launch traced here: 55.7 us
  Pallas kernels  55.1 us (98%)
  between operations  0.64 us (1%)
    pallas_call x1, Pallas kernels, body(): pl.pallas_call(kernel, out_shape=(jax.ShapeDtypeStruct((1, 3, ROWS, NX, N...  53 us
    pallas_call x1, Pallas kernels, body(): pl.pallas_call(write_out, out_shape=[jax.ShapeDtypeStruct(x.shape, x.dtyp...  2.11 us

profile of v3, /device:TPU:33, one launch (start us, length us, event | category | flops | bytes accessed | tf_op | source)
XLA Modules:
  0.0 55.7 jit_solution(8687917914171171062)
XLA Ops:
  0.6 53.0 %shard_map.139 = (f32[1,3,8,16,512]{4,3,2,1,0:T(8,128)}, f32[1,8,16,512]{3,2,1,0:T(8,128)}, f32[1,128]{1,0:T(1,128)}) custom-call(f32[1,3,8,16,512]{4,3,2,1,0:T(8,128)} %vel.1, f32[1,3,8,512]{3,2,1,0:T(8,128)} %prec.1, s32[1,8,512]{2,1,0:T(8,128)} %rot.1, s32[1,256]{1,0:T(1,128)} %fcell_hbm.1, s32[1,256]{1,0:T(1,128)} %bitcast.1, s32[1,256]{1,0:T(1,128)} %fpan_hbm.1, ...), custom_call_target="tpu_custom_call" | custom-call | tf_op jit(solution)/shard_map/pallas_call | solution.py:566
  53.6 2.1 %shard_map.140 = (f32[1,3,8,16,512]{4,3,2,1,0:T(8,128)}, f32[1,8,16,512]{3,2,1,0:T(8,128)}, f32[1,128]{1,0:T(1,128)}) custom-call(f32[1,3,8,16,512]{4,3,2,1,0:T(8,128)} %get-tuple-element.6.vel, f32[1,8,16,512]{3,2,1,0:T(8,128)} %get-tuple-element.7.pot, f32[1,128]{1,0:T(1,128)} %get-tuple-element.8.force), custom_call_target="tpu_custom_call" | custom-call | tf_op jit(solution)/shard_map/pallas_call | solution.py:617

commit v4 on v3

--- a/solution.py
+++ b/solution.py
@@ -143,8 +143,9 @@
         for k in range(GROUP):
             pl.semaphore_signal(barrier, inc=1, device_id=(1, (s + k) % GROUP), device_id_type=MESH)
         pl.semaphore_wait(barrier, DIRS - 1)
-        for k in range(1, DIRS):
-            remote(prec.at[0], pb, s_p.at[k], r_p, (k, s)).start()
+        for c in range(3):
+            for k in range(1, DIRS):
+                remote(prec.at[0, c], pb.at[c], s_p.at[c, k], r_p.at[c], (k, s)).start()
         own = pltpu.make_async_copy(prec.at[0], pb, l_p)
         own.start()
         own.wait()
@@ -185,12 +186,12 @@
         for a, b in lists:
             remote(a, b.at[j], s_c, r_c, (d, 4 * zc + (j + dk) % 4)).start()
 
-    @pl.when(d != 0)
-    def _():
-        remote(prec.at[0], pb, s_p.at[0], r_p, (0, s)).wait_recv()
-
     for t in range(TILES):
         c, k = t // 4, t % 4
+
+        @pl.when((d != 0) & (k == 0))
+        def _(c=c):
+            remote(prec.at[0, c], pb.at[c], s_p.at[c, 0], r_p.at[c], (0, s)).wait_recv()
 
         @pl.when(s != owners[t])
         def _(t=t, c=c, k=k):
@@ -423,15 +424,20 @@
     for dk in (2, 3, 1, 0):
         first = 8 * (j ^ dk)
 
-        def filter_row(y, carry, first=first, dk=dk):
-            at = first + y + HALO - 1
-            total = taps[0] * win[at]
+        def filter_pair(y, carry, first=first, dk=dk):
+            at = first + 2 * y + HALO - 1
+            near = {0: win[at], 1: win[at + 1]}
+            one, two = taps[0] * near[0], taps[0] * near[1]
             for i in range(1, ITERS):
-                total = total + taps[i] * (win[at + i] + win[at - i])
-            ph[dk, y] = total
+                near[1 + i], near[-i] = win[at + 1 + i], win[at - i]
+                tap = taps[i]
+                one = one + tap * (near[i] + near[-i])
+                two = two + tap * (near[1 + i] + near[1 - i])
+            ph[dk, 2 * y] = one
+            ph[dk, 2 * y + 1] = two
             return carry
 
-        lax.fori_loop(0, ROWS + 2, filter_row, 0)
+        lax.fori_loop(0, ROWS // 2 + 1, filter_pair, 0)
         if dk:
             back = remote(ph.at[dk], bk.at[dk], s_b.at[dk], r_b.at[dk], (d, 4 * zc + (j ^ dk)))
             back.start()
@@ -490,8 +496,9 @@
 
     @pl.when(d == 0)
     def _():
-        for k in range(1, DIRS):
-            remote(prec.at[0], pb, s_p.at[k], r_p, (k, s)).wait_send()
+        for c in range(3):
+            for k in range(1, DIRS):
+                remote(prec.at[0, c], pb.at[c], s_p.at[c, k], r_p.at[c], (k, s)).wait_send()
 
     eight = pl.ds(0, 8 * (TILES - 1))
 
@@ -605,8 +612,8 @@
             pltpu.VMEM((4, FACADES, 128), f32),
             pltpu.VMEM((4, FACADES, 128), f32),
             pltpu.VMEM((4, GROUP, FACADES), f32),
-            dma((10,)), pltpu.SemaphoreType.REGULAR, dma((4,)), dma((4,)), dma((DIRS,)),
-            dma, dma, dma, dma, dma, dma, dma, dma, dma, dma, dma, dma((4,)), dma((4,)), dma, dma, dma, dma, dma, dma((2,)),
+            dma((10,)), pltpu.SemaphoreType.REGULAR, dma((4,)), dma((4,)), dma((3, DIRS)),
+            dma((3,)), dma, dma, dma, dma, dma, dma, dma, dma, dma, dma, dma((4,)), dma((4,)), dma, dma, dma, dma, dma, dma((2,)),
         ],
         compiler_params=pltpu.CompilerParams(
             collective_id=0, has_side_effects=True, vmem_limit_bytes=60 << 20

time: 56 us -> 54.6 us (0.975)
  Pallas kernels: 55.1 us -> 53.6 us
    pallas_call x1, Pallas kernels: 53 us -> 51.5 us  [body(): pl.pallas_call(kernel, out_shape=(jax.ShapeDtypeStruct((1, 3, ROWS, NX, N...]
where the time goes in v4:
time: 54.6 us; the launch traced here: 54.2 us
  Pallas kernels  53.6 us (98%)
  between operations  0.64 us (1%)
    pallas_call x1, Pallas kernels, body(): pl.pallas_call(kernel, out_shape=(jax.ShapeDtypeStruct((1, 3, ROWS, NX, N...  51.5 us
    pallas_call x1, Pallas kernels, body(): pl.pallas_call(write_out, out_shape=[jax.ShapeDtypeStruct(x.shape, x.dtyp...  2.11 us

profile of v4, /device:TPU:33, one launch (start us, length us, event | category | flops | bytes accessed | tf_op | source)
XLA Modules:
  0.0 54.2 jit_solution(16347528775194691989)
XLA Ops:
  0.6 51.5 %shard_map.139 = (f32[1,3,8,16,512]{4,3,2,1,0:T(8,128)}, f32[1,8,16,512]{3,2,1,0:T(8,128)}, f32[1,128]{1,0:T(1,128)}) custom-call(f32[1,3,8,16,512]{4,3,2,1,0:T(8,128)} %vel.1, f32[1,3,8,512]{3,2,1,0:T(8,128)} %prec.1, s32[1,8,512]{2,1,0:T(8,128)} %rot.1, s32[1,256]{1,0:T(1,128)} %fcell_hbm.1, s32[1,256]{1,0:T(1,128)} %bitcast.1, s32[1,256]{1,0:T(1,128)} %fpan_hbm.1, ...), custom_call_target="tpu_custom_call" | custom-call | tf_op jit(solution)/shard_map/pallas_call | solution.py:573
  52.1 2.1 %shard_map.140 = (f32[1,3,8,16,512]{4,3,2,1,0:T(8,128)}, f32[1,8,16,512]{3,2,1,0:T(8,128)}, f32[1,128]{1,0:T(1,128)}) custom-call(f32[1,3,8,16,512]{4,3,2,1,0:T(8,128)} %get-tuple-element.6.vel, f32[1,8,16,512]{3,2,1,0:T(8,128)} %get-tuple-element.7.pot, f32[1,128]{1,0:T(1,128)} %get-tuple-element.8.force), custom_call_target="tpu_custom_call" | custom-call | tf_op jit(solution)/shard_map/pallas_call | solution.py:624
